TPU v7x, 256 devices: a whole 4x4x8 slice. The times are simulated.
256 devices in a mesh: ctx: 8 (over z), head: 4 (over x_hi, core), dp: 8 (over x_lo, y).
Axes of the slice: x: 4 (x_hi: 2, x_lo: 2; x = x_hi * 2 + x_lo), y: 4, z: 8, core: 2. Of those that a mesh axis runs over, the one named last changes fastest.
Arguments:
- query: bfloat16 [22528, 5120], P(('ctx', 'dp'), 'head'), may hold values from -4 to 4
- keys: bfloat16 [22528, 1024], P(('ctx', 'dp'), 'head'), may hold values from -4 to 4
- values: bfloat16 [22528, 1024], P(('ctx', 'dp'), 'head'), may hold values from -4 to 4
- output: bfloat16 [22528, 5120], P(('ctx', 'dp'), 'head'), may hold values from -3 to 3
- grad_out: bfloat16 [22528, 5120], P(('ctx', 'dp'), 'head'), may hold values from -4 to 4
- log_norm: bfloat16 [22528, 40], P(('ctx', 'dp'), 'head'), may hold values from 4 to 7
- route_counts: int32 [64, 64], replicated, may hold values from 0 to 11, as said below
- doc_lengths: int32 [8, 4], P('dp'), may hold values from 1 to 1408, 2816 in all within a row
Outputs:
- grad_query: bfloat16 [22528, 5120], P(('ctx', 'dp'), 'head')
- grad_key: bfloat16 [22528, 1024], P(('ctx', 'dp'), 'head')
- grad_value: bfloat16 [22528, 1024], P(('ctx', 'dp'), 'head')
Inputs may be any that keep to these rules, and one draw needn't show every extreme that they name: Every row and every column of route_counts sums to 352; some entries equal 11 in every draw.
All inputs are finite; a program needn't handle non-finite values.
Results may differ from a plain program's by a relative error of at most 0.0051.
Values may be sent and summed in bfloat16 or wider, within the bound.
A program may use at most 192 MiB of HBM per device.

v0:
```python
import jax
import jax.numpy as jnp
from jax import lax
from jax.sharding import PartitionSpec as P

HDIM = 128


def as_sent(array):

    def short(part):
        return part.astype(jnp.bfloat16) if part.dtype == jnp.float32 else part

    return jax.tree.map(short, array)


def passed_along(array, axis, by):
    peers = lax.axis_size(axis)
    pairs = [(i, i + by) for i in range(peers) if 0 <= i + by < peers]
    return lax.ppermute(array, axis, pairs)


def shifted(value, axis, steps):
    count = lax.axis_size(axis)
    pairs = [(source, (source + steps) % count) for source in range(count)]
    return lax.ppermute(value, axis, pairs)


def pack_rows(arrays, counts_vec, capacity):
    starts = jnp.cumsum(counts_vec) - counts_vec
    within = jnp.arange(capacity, dtype=jnp.int32)
    source_rows = (starts[:, None] + within[None, :]).reshape(-1)
    valid = (within[None, :] < counts_vec[:, None]).reshape(-1)
    picked = jnp.clip(source_rows, 0, arrays[0].shape[0] - 1)
    return tuple(
        (
            jnp.where(valid[:, None], member[picked], jnp.zeros((), member.dtype))
            for member in arrays
        )
    )


def place_rows(arrays, counts_vec, capacity, tok_rows):
    ends = jnp.cumsum(counts_vec)
    starts = ends - counts_vec
    row_ids = jnp.arange(tok_rows, dtype=jnp.int32)
    source = jnp.sum((ends[None, :] <= row_ids[:, None]).astype(jnp.int32), axis=1)
    chosen = jnp.arange(counts_vec.shape[0], dtype=jnp.int32)[None, :] == source[:, None]
    offset = row_ids - jnp.sum(jnp.where(chosen, starts[None, :], 0), axis=1)
    picked = source * capacity + offset
    return tuple((member[picked] for member in arrays))


def response_ids(positions, lengths_row):
    bounds = jnp.cumsum(lengths_row)
    return jnp.sum((bounds[None, :] <= positions[:, None]).astype(jnp.int32), axis=1)


def head_delta(grad_rows, out_rows, heads_local):
    products = grad_rows.astype(jnp.float32) * out_rows.astype(jnp.float32)
    return jnp.sum(products.reshape(grad_rows.shape[0], heads_local, HDIM), axis=2).astype(
        jnp.bfloat16
    )


def tile_grads(queries, grad_rows, delta, log_norm, visible, key_rows, value_rows, kv_heads):
    tq = queries.shape[0]
    tk = key_rows.shape[0]
    group = queries.shape[1] // (kv_heads * HDIM)
    scale = HDIM ** (-0.5)
    q_four = queries.reshape(tq, kv_heads, group, HDIM)
    g_four = grad_rows.reshape(tq, kv_heads, group, HDIM)
    k_three = key_rows.reshape(tk, kv_heads, HDIM)
    v_three = value_rows.reshape(tk, kv_heads, HDIM)
    scores = (
        jnp.einsum("qgrd,kgd->grqk", q_four, k_three, preferred_element_type=jnp.float32) * scale
    )
    lse_four = (
        log_norm.astype(jnp.float32).reshape(tq, kv_heads, group).transpose(1, 2, 0)[..., None]
    )
    probs = jnp.where(visible[None, None], jnp.exp(scores - lse_four), 0.0)
    probs_low = probs.astype(jnp.bfloat16)
    dvalues = jnp.einsum("grqk,qgrd->kgd", probs_low, g_four, preferred_element_type=jnp.float32)
    dprob = jnp.einsum("qgrd,kgd->grqk", g_four, v_three, preferred_element_type=jnp.float32)
    delta_four = delta.reshape(tq, kv_heads, group).transpose(1, 2, 0)[..., None]
    dscore = (probs * (dprob - delta_four) * scale).astype(jnp.bfloat16)
    dquery = jnp.einsum("grqk,kgd->qgrd", dscore, k_three, preferred_element_type=jnp.float32)
    dkeys = jnp.einsum("grqk,qgrd->kgd", dscore, q_four, preferred_element_type=jnp.float32)
    return (dquery.reshape(tq, -1), dkeys.reshape(tk, -1), dvalues.reshape(tk, -1))


def body(query, keys, values, output, grad_out, log_norm, route_counts, doc_lengths):
    owners = lax.axis_size(("ctx", "dp"))
    rank = lax.axis_index(("ctx", "dp"))
    ctx_count = lax.axis_size("ctx")
    ctx_rank = lax.axis_index("ctx")
    tok_rows = query.shape[0]
    capacity = 2 * tok_rows // owners
    kv_local = keys.shape[1] // HDIM
    heads_local = query.shape[1] // HDIM
    send_counts = lax.dynamic_index_in_dim(route_counts, rank, 0, keepdims=False)
    recv_counts = lax.dynamic_index_in_dim(route_counts, rank, 1, keepdims=False)
    packed = pack_rows((query, keys, values, output, grad_out, log_norm), send_counts, capacity)
    arrived = jax.tree.map(
        lambda part, own: part.astype(own.dtype),
        lax.all_to_all(as_sent(packed), ("ctx", "dp"), split_axis=0, concat_axis=0, tiled=True),
        packed,
    )
    q_ctx, k_ctx, v_ctx, o_ctx, g_ctx, l_ctx = place_rows(arrived, recv_counts, capacity, tok_rows)
    d_ctx = lax.optimization_barrier(head_delta(g_ctx, o_ctx, heads_local))
    delta = d_ctx.astype(jnp.float32)
    lengths_row = doc_lengths[0]
    query_pos = ctx_rank * tok_rows + jnp.arange(tok_rows, dtype=jnp.int32)
    query_doc = response_ids(query_pos, lengths_row)

    def block_terms(key_rows, value_rows, key_pos):
        key_doc = response_ids(key_pos, lengths_row)
        visible = (key_pos[None, :] <= query_pos[:, None]) & (
            key_doc[None, :] == query_doc[:, None]
        )
        return tile_grads(q_ctx, g_ctx, delta, l_ctx, visible, key_rows, value_rows, kv_local)

    def pass_step(step, carry):
        key_blk, val_blk, dkey_acc, dval_acc, dquery_acc = carry
        anchor = (ctx_rank - step) % ctx_count
        key_pos = anchor * tok_rows + jnp.arange(tok_rows, dtype=jnp.int32)
        dquery_part, dkey_part, dval_part = block_terms(key_blk, val_blk, key_pos)
        dquery_acc = dquery_acc + dquery_part
        dkey_acc = dkey_acc + dkey_part
        dval_acc = dval_acc + dval_part
        key_blk, val_blk = passed_along((key_blk, val_blk), "ctx", 1)
        dkey_acc, dval_acc = shifted((dkey_acc, dval_acc), "ctx", 1)
        return (key_blk, val_blk, dkey_acc, dval_acc, dquery_acc)

    blank_kv = jnp.zeros(k_ctx.shape, jnp.float32)
    start_carry = (k_ctx, v_ctx, blank_kv, blank_kv, jnp.zeros(q_ctx.shape, jnp.float32))
    final_carry = lax.fori_loop(0, ctx_count, pass_step, start_carry)
    dkey_acc, dval_acc, dquery_acc = (final_carry[2], final_carry[3], final_carry[4])
    back_q, back_k, back_v = pack_rows(
        (
            dquery_acc.astype(jnp.bfloat16),
            dkey_acc.astype(jnp.bfloat16),
            dval_acc.astype(jnp.bfloat16),
        ),
        recv_counts,
        capacity,
    )
    returned = (
        lax.all_to_all(back_q, ("ctx", "dp"), split_axis=0, concat_axis=0, tiled=True),
        lax.all_to_all(back_k, ("ctx", "dp"), split_axis=0, concat_axis=0, tiled=True),
        lax.all_to_all(back_v, ("ctx", "dp"), split_axis=0, concat_axis=0, tiled=True),
    )
    grad_query, grad_key, grad_value = place_rows(returned, send_counts, capacity, tok_rows)
    return (grad_query, grad_key, grad_value)


def solution(mesh):
    in_specs = (
        P(("ctx", "dp"), "head"),
        P(("ctx", "dp"), "head"),
        P(("ctx", "dp"), "head"),
        P(("ctx", "dp"), "head"),
        P(("ctx", "dp"), "head"),
        P(("ctx", "dp"), "head"),
        P(),
        P("dp", None),
    )
    out_specs = (P(("ctx", "dp"), "head"), P(("ctx", "dp"), "head"), P(("ctx", "dp"), "head"))
    return jax.shard_map(body, mesh=mesh, in_specs=in_specs, out_specs=out_specs, check_vma=False)
```

profile of v0, /device:TPU:4, one launch (start us, length us, event | category | flops | bytes accessed | tf_op | source)
XLA Modules:
  0.0 661.0 jit_solution(15609757954329769970)
XLA Ops:
  7.7 12.7 %all-to-all-start.3 = ((bf16[64,11,10]{1,2,0:T(8,128)(2,1)}), bf16[64,11,10]{1,2,0:T(8,128)(2,1)S(1)}, u32[]{:S(2)}, u32[]{:S(2)}) async-start(bf16[64,11,10]{1,2,0:T(8,128)(2,1)} %copy.78), calls=%async_computation.3 | async-start | bytes 524288 | tf_op jit(solution)/shard_map/all_to_all | solution.py:106
  27.6 6.0 all-to-all-done.3
  33.6 5.2 all-to-all-start.1
  56.4 10.0 %all-to-all-start = ((bf16[64,11,256]{2,1,0:T(8,128)(2,1)}), bf16[64,11,256]{2,1,0:T(8,128)(2,1)}, u32[]{:S(2)}, u32[]{:S(2)}) async-start(bf16[64,11,256]{2,1,0:T(8,128)(2,1)} %get-tuple-element.482), calls=%async_computation | async-start | bytes 1048576 | tf_op jit(solution)/shard_map/all_to_all | solution.py:106
  66.4 5.2 broadcast_select_fusion
  71.6 11.8 %all-to-all-done = bf16[64,11,256]{2,1,0:T(8,128)(2,1)} async-done(((bf16[64,11,256]{2,1,0:T(8,128)(2,1)}), bf16[64,11,256]{2,1,0:T(8,128)(2,1)}, u32[]{:S(2)}, u32[]{:S(2)}) %all-to-all-start) | async-done | bytes 360480 | tf_op jit(solution)/shard_map/all_to_all | solution.py:106
  83.3 67.5 %all_to_all.81 = bf16[64,11,1280]{2,1,0:T(8,128)(2,1)} all-to-all(bf16[64,11,1280]{2,1,0:T(8,128)(2,1)} %get-tuple-element.478), channel_id=1, replica_groups=mesh['ctx'=8,'head'=4,'dp'=8] {'ctx','dp'}, dimensions={0} | all-to-all | bytes 3604480 | tf_op jit(solution)/shard_map/all_to_all | solution.py:106
  150.8 67.0 %all_to_all.82 = bf16[64,11,1280]{2,1,0:T(8,128)(2,1)} all-to-all(bf16[64,11,1280]{2,1,0:T(8,128)(2,1)S(1)} %get-tuple-element.479), channel_id=1, replica_groups=mesh['ctx'=8,'head'=4,'dp'=8] {'ctx','dp'}, dimensions={0} | all-to-all | bytes 3604480 | tf_op jit(solution)/shard_map/all_to_all | solution.py:106
  217.8 6.2 all-to-all-start.2
  244.0 40.2 %all-to-all-done.2 = bf16[64,11,1280]{2,1,0:T(8,128)(2,1)} async-done(((bf16[64,11,1280]{2,1,0:T(8,128)(2,1)}), bf16[64,11,1280]{2,1,0:T(8,128)(2,1)}, u32[]{:S(2)}, u32[]{:S(2)}) %all-to-all-start.2) | async-done | bytes 1802272 | tf_op jit(solution)/shard_map/all_to_all | solution.py:106
  298.9 248.4 %while.25 = (s32[]{:T(128)}, bf16[352,256]{1,0:T(8,128)(2,1)}, bf16[352,256]{1,0:T(8,128)(2,1)S(1)}, f32[352,256]{1,0:T(8,128)}, f32[352,256]{1,0:T(8,128)}, /*i...) while((s32[]{:T(128)}, bf16[352,256]{1,0:T(8,128)(2,1)}, ...), condition=%wide.wide.region_10.11_spmd.clone, body=%wide.wide.region_8.10_spmd.clone.sunk | while | flops 1601058304 | bytes 50684336 | solution.py:137
  327.3 3.9 collective-permute-done.3
  364.9 3.3 collective-permute-start
  412.5 3.5 collective-permute-start.3
  425.0 3.7 collective-permute-start
  428.7 3.7 collective-permute-start.1
  516.2 3.9 collective-permute-start
  552.3 3.3 gather_fusion.16
  557.8 22.1 %all_to_all.83 = bf16[64,11,256]{2,1,0:T(8,128)(2,1)} all-to-all(bf16[64,11,256]{2,1,0:T(8,128)(2,1)S(1)} %get-tuple-element.476), channel_id=1, replica_groups=mesh['ctx'=8,'head'=4,'dp'=8] {'ctx','dp'}, dimensions={0} | all-to-all | bytes 720896 | tf_op jit(solution)/shard_map/all_to_all | solution.py:151
  579.9 6.4 all-to-all-start.7
  587.0 3.7 gather_fusion.12
  595.0 5.4 all-to-all-done.7
  600.5 8.1 %all-to-all-start.6 = ((bf16[64,11,1280]{2,1,0:T(8,128)(2,1)}), bf16[64,11,1280]{2,1,0:T(8,128)(2,1)}, u32[]{:S(2)}, u32[]{:S(2)}) async-start(bf16[64,11,1280]{2,1,0:T(8,128)(2,1)} %broadcast_select_fusion.3), calls=%async_computation.6 | async-start | bytes 5242880 | tf_op jit(solution)/shard_map/all_to_all | solution.py:149
  614.2 40.9 %all-to-all-done.6 = bf16[64,11,1280]{2,1,0:T(8,128)(2,1)} async-done(((bf16[64,11,1280]{2,1,0:T(8,128)(2,1)}), bf16[64,11,1280]{2,1,0:T(8,128)(2,1)}, u32[]{:S(2)}, u32[]{:S(2)}) %all-to-all-start.6) | async-done | bytes 1802272 | tf_op jit(solution)/shard_map/all_to_all | solution.py:149
  (351 shorter events, 314.8 us)
Async XLA Ops:
  7.7 25.9 %all-to-all-start.3 = ((bf16[64,11,10]{1,2,0:T(8,128)(2,1)}), bf16[64,11,10]{1,2,0:T(8,128)(2,1)S(1)}, u32[]{:S(2)}, u32[]{:S(2)}) async-start(bf16[64,11,10]{1,2,0:T(8,128)(2,1)} %copy.78), calls=%async_computation.3 | async-start | bytes 524288 | tf_op jit(solution)/shard_map/all_to_all | solution.py:106
  33.6 22.7 %all-to-all-start.1 = ((bf16[64,11,256]{2,1,0:T(8,128)(2,1)}), bf16[64,11,256]{2,1,0:T(8,128)(2,1)S(1)}, u32[]{:S(2)}, u32[]{:S(2)}) async-start(bf16[64,11,256]{2,1,0:T(8,128)(2,1)} %get-tuple-element.481), calls=%async_computation.1 | async-start | bytes 1048576 | tf_op jit(solution)/shard_map/all_to_all | solution.py:106
  56.4 27.0 %all-to-all-start = ((bf16[64,11,256]{2,1,0:T(8,128)(2,1)}), bf16[64,11,256]{2,1,0:T(8,128)(2,1)}, u32[]{:S(2)}, u32[]{:S(2)}) async-start(bf16[64,11,256]{2,1,0:T(8,128)(2,1)} %get-tuple-element.482), calls=%async_computation | async-start | bytes 1048576 | tf_op jit(solution)/shard_map/all_to_all | solution.py:106
  217.8 66.4 %all-to-all-start.2 = ((bf16[64,11,1280]{2,1,0:T(8,128)(2,1)}), bf16[64,11,1280]{2,1,0:T(8,128)(2,1)}, u32[]{:S(2)}, u32[]{:S(2)}) async-start(bf16[64,11,1280]{2,1,0:T(8,128)(2,1)} %get-tuple-element.480), calls=%async_computation.2 | async-start | bytes 5242880 | tf_op jit(solution)/shard_map/all_to_all | solution.py:106
  300.0 25.9 %collective-permute-start = (bf16[352,256]{1,0:T(8,128)(2,1)S(1)}, bf16[352,256]{1,0:T(8,128)(2,1)}, u32[]{:S(2)}, u32[]{:S(2)}) collective-permute-start(bf16[352,256]{1,0:T(8,128)(2,1)S(1)} %copy.137), channel_id=1, source_target_pairs={{0,32},{32,64},{64,96},{96,128},{128,160},{160,192},{192,224},{1,3... | collective-permute-start | bytes 540680 | tf_op jit(solution)/shard_map/while/body/eval_jaxpr/ppermute | solution.py:20
  303.3 22.7 %collective-permute-start.1 = (bf16[352,256]{1,0:T(8,128)(2,1)S(1)}, bf16[352,256]{1,0:T(8,128)(2,1)S(1)}, u32[]{:S(2)}, u32[]{:S(2)}) collective-permute-start(bf16[352,256]{1,0:T(8,128)(2,1)S(1)} %copy.138), channel_id=1, source_target_pairs={{0,32},{32,64},{64,96},{96,128},{128,160},{160,192},{192,224},{1,3... | collective-permute-start | bytes 540680 | tf_op jit(solution)/shard_map/while/body/eval_jaxpr/ppermute | solution.py:20
  332.1 29.6 %collective-permute-start = (bf16[352,256]{1,0:T(8,128)(2,1)S(1)}, bf16[352,256]{1,0:T(8,128)(2,1)}, u32[]{:S(2)}, u32[]{:S(2)}) collective-permute-start(bf16[352,256]{1,0:T(8,128)(2,1)S(1)} %copy.137), channel_id=1, source_target_pairs={{0,32},{32,64},{64,96},{96,128},{128,160},{160,192},{192,224},{1,3... | collective-permute-start | bytes 540680 | tf_op jit(solution)/shard_map/while/body/eval_jaxpr/ppermute | solution.py:20
  334.6 27.1 %collective-permute-start.1 = (bf16[352,256]{1,0:T(8,128)(2,1)S(1)}, bf16[352,256]{1,0:T(8,128)(2,1)S(1)}, u32[]{:S(2)}, u32[]{:S(2)}) collective-permute-start(bf16[352,256]{1,0:T(8,128)(2,1)S(1)} %copy.138), channel_id=1, source_target_pairs={{0,32},{32,64},{64,96},{96,128},{128,160},{160,192},{192,224},{1,3... | collective-permute-start | bytes 540680 | tf_op jit(solution)/shard_map/while/body/eval_jaxpr/ppermute | solution.py:20
  364.9 26.9 %collective-permute-start = (bf16[352,256]{1,0:T(8,128)(2,1)S(1)}, bf16[352,256]{1,0:T(8,128)(2,1)}, u32[]{:S(2)}, u32[]{:S(2)}) collective-permute-start(bf16[352,256]{1,0:T(8,128)(2,1)S(1)} %copy.137), channel_id=1, source_target_pairs={{0,32},{32,64},{64,96},{96,128},{128,160},{160,192},{192,224},{1,3... | collective-permute-start | bytes 540680 | tf_op jit(solution)/shard_map/while/body/eval_jaxpr/ppermute | solution.py:20
  368.2 23.6 %collective-permute-start.1 = (bf16[352,256]{1,0:T(8,128)(2,1)S(1)}, bf16[352,256]{1,0:T(8,128)(2,1)S(1)}, u32[]{:S(2)}, u32[]{:S(2)}) collective-permute-start(bf16[352,256]{1,0:T(8,128)(2,1)S(1)} %copy.138), channel_id=1, source_target_pairs={{0,32},{32,64},{64,96},{96,128},{128,160},{160,192},{192,224},{1,3... | collective-permute-start | bytes 540680 | tf_op jit(solution)/shard_map/while/body/eval_jaxpr/ppermute | solution.py:20
  395.5 27.9 %collective-permute-start = (bf16[352,256]{1,0:T(8,128)(2,1)S(1)}, bf16[352,256]{1,0:T(8,128)(2,1)}, u32[]{:S(2)}, u32[]{:S(2)}) collective-permute-start(bf16[352,256]{1,0:T(8,128)(2,1)S(1)} %copy.137), channel_id=1, source_target_pairs={{0,32},{32,64},{64,96},{96,128},{128,160},{160,192},{192,224},{1,3... | collective-permute-start | bytes 540680 | tf_op jit(solution)/shard_map/while/body/eval_jaxpr/ppermute | solution.py:20
  397.5 26.0 %collective-permute-start.1 = (bf16[352,256]{1,0:T(8,128)(2,1)S(1)}, bf16[352,256]{1,0:T(8,128)(2,1)S(1)}, u32[]{:S(2)}, u32[]{:S(2)}) collective-permute-start(bf16[352,256]{1,0:T(8,128)(2,1)S(1)} %copy.138), channel_id=1, source_target_pairs={{0,32},{32,64},{64,96},{96,128},{128,160},{160,192},{192,224},{1,3... | collective-permute-start | bytes 540680 | tf_op jit(solution)/shard_map/while/body/eval_jaxpr/ppermute | solution.py:20
  408.8 14.6 %collective-permute-start.2 = (f32[352,256]{1,0:T(8,128)}, f32[352,256]{1,0:T(8,128)}, u32[]{:S(2)}, u32[]{:S(2)}) collective-permute-start(f32[352,256]{1,0:T(8,128)} %bitcast_add_fusion.9), channel_id=1, source_target_pairs={{0,32},{32,64},{64,96},{96,128},{128,160},{160,192},{192,224},{224... | collective-permute-start | bytes 1081352 | tf_op jit(solution)/shard_map/while/body/eval_jaxpr/ppermute | solution.py:26
  425.0 29.5 %collective-permute-start = (bf16[352,256]{1,0:T(8,128)(2,1)S(1)}, bf16[352,256]{1,0:T(8,128)(2,1)}, u32[]{:S(2)}, u32[]{:S(2)}) collective-permute-start(bf16[352,256]{1,0:T(8,128)(2,1)S(1)} %copy.137), channel_id=1, source_target_pairs={{0,32},{32,64},{64,96},{96,128},{128,160},{160,192},{192,224},{1,3... | collective-permute-start | bytes 540680 | tf_op jit(solution)/shard_map/while/body/eval_jaxpr/ppermute | solution.py:20
  428.7 25.8 %collective-permute-start.1 = (bf16[352,256]{1,0:T(8,128)(2,1)S(1)}, bf16[352,256]{1,0:T(8,128)(2,1)S(1)}, u32[]{:S(2)}, u32[]{:S(2)}) collective-permute-start(bf16[352,256]{1,0:T(8,128)(2,1)S(1)} %copy.138), channel_id=1, source_target_pairs={{0,32},{32,64},{64,96},{96,128},{128,160},{160,192},{192,224},{1,3... | collective-permute-start | bytes 540680 | tf_op jit(solution)/shard_map/while/body/eval_jaxpr/ppermute | solution.py:20
  457.6 26.1 %collective-permute-start = (bf16[352,256]{1,0:T(8,128)(2,1)S(1)}, bf16[352,256]{1,0:T(8,128)(2,1)}, u32[]{:S(2)}, u32[]{:S(2)}) collective-permute-start(bf16[352,256]{1,0:T(8,128)(2,1)S(1)} %copy.137), channel_id=1, source_target_pairs={{0,32},{32,64},{64,96},{96,128},{128,160},{160,192},{192,224},{1,3... | collective-permute-start | bytes 540680 | tf_op jit(solution)/shard_map/while/body/eval_jaxpr/ppermute | solution.py:20
  459.6 24.1 %collective-permute-start.1 = (bf16[352,256]{1,0:T(8,128)(2,1)S(1)}, bf16[352,256]{1,0:T(8,128)(2,1)S(1)}, u32[]{:S(2)}, u32[]{:S(2)}) collective-permute-start(bf16[352,256]{1,0:T(8,128)(2,1)S(1)} %copy.138), channel_id=1, source_target_pairs={{0,32},{32,64},{64,96},{96,128},{128,160},{160,192},{192,224},{1,3... | collective-permute-start | bytes 540680 | tf_op jit(solution)/shard_map/while/body/eval_jaxpr/ppermute | solution.py:20
  486.1 29.1 %collective-permute-start = (bf16[352,256]{1,0:T(8,128)(2,1)S(1)}, bf16[352,256]{1,0:T(8,128)(2,1)}, u32[]{:S(2)}, u32[]{:S(2)}) collective-permute-start(bf16[352,256]{1,0:T(8,128)(2,1)S(1)} %copy.137), channel_id=1, source_target_pairs={{0,32},{32,64},{64,96},{96,128},{128,160},{160,192},{192,224},{1,3... | collective-permute-start | bytes 540680 | tf_op jit(solution)/shard_map/while/body/eval_jaxpr/ppermute | solution.py:20
  489.0 26.2 %collective-permute-start.1 = (bf16[352,256]{1,0:T(8,128)(2,1)S(1)}, bf16[352,256]{1,0:T(8,128)(2,1)S(1)}, u32[]{:S(2)}, u32[]{:S(2)}) collective-permute-start(bf16[352,256]{1,0:T(8,128)(2,1)S(1)} %copy.138), channel_id=1, source_target_pairs={{0,32},{32,64},{64,96},{96,128},{128,160},{160,192},{192,224},{1,3... | collective-permute-start | bytes 540680 | tf_op jit(solution)/shard_map/while/body/eval_jaxpr/ppermute | solution.py:20
  516.2 31.1 %collective-permute-start = (bf16[352,256]{1,0:T(8,128)(2,1)S(1)}, bf16[352,256]{1,0:T(8,128)(2,1)}, u32[]{:S(2)}, u32[]{:S(2)}) collective-permute-start(bf16[352,256]{1,0:T(8,128)(2,1)S(1)} %copy.137), channel_id=1, source_target_pairs={{0,32},{32,64},{64,96},{96,128},{128,160},{160,192},{192,224},{1,3... | collective-permute-start | bytes 540680 | tf_op jit(solution)/shard_map/while/body/eval_jaxpr/ppermute | solution.py:20
  520.1 27.2 %collective-permute-start.1 = (bf16[352,256]{1,0:T(8,128)(2,1)S(1)}, bf16[352,256]{1,0:T(8,128)(2,1)S(1)}, u32[]{:S(2)}, u32[]{:S(2)}) collective-permute-start(bf16[352,256]{1,0:T(8,128)(2,1)S(1)} %copy.138), channel_id=1, source_target_pairs={{0,32},{32,64},{64,96},{96,128},{128,160},{160,192},{192,224},{1,3... | collective-permute-start | bytes 540680 | tf_op jit(solution)/shard_map/while/body/eval_jaxpr/ppermute | solution.py:20
  532.7 14.6 %collective-permute-start.2 = (f32[352,256]{1,0:T(8,128)}, f32[352,256]{1,0:T(8,128)}, u32[]{:S(2)}, u32[]{:S(2)}) collective-permute-start(f32[352,256]{1,0:T(8,128)} %bitcast_add_fusion.9), channel_id=1, source_target_pairs={{0,32},{32,64},{64,96},{96,128},{128,160},{160,192},{192,224},{224... | collective-permute-start | bytes 1081352 | tf_op jit(solution)/shard_map/while/body/eval_jaxpr/ppermute | solution.py:26
  579.9 20.5 %all-to-all-start.7 = ((bf16[64,11,256]{2,1,0:T(8,128)(2,1)}), bf16[64,11,256]{2,1,0:T(8,128)(2,1)S(1)}, u32[]{:S(2)}, u32[]{:S(2)}) async-start(bf16[64,11,256]{2,1,0:T(8,128)(2,1)} %get-tuple-element.477), calls=%async_computation.7 | async-start | bytes 1048576 | tf_op jit(solution)/shard_map/all_to_all | solution.py:150
  600.5 54.7 %all-to-all-start.6 = ((bf16[64,11,1280]{2,1,0:T(8,128)(2,1)}), bf16[64,11,1280]{2,1,0:T(8,128)(2,1)}, u32[]{:S(2)}, u32[]{:S(2)}) async-start(bf16[64,11,1280]{2,1,0:T(8,128)(2,1)} %broadcast_select_fusion.3), calls=%async_computation.6 | async-start | bytes 5242880 | tf_op jit(solution)/shard_map/all_to_all | solution.py:149
  (42 other events, 350.7 us)
where the time goes:
time: 674 us; the launch traced here: 661 us
  blocking collectives  157 us (23%)
  waiting for transfers between devices  120 us (18%)
  local copies, waits for them, and re-layouts  114 us (17%)
  starting transfers between devices  114 us (17%)
  matrix products  84.4 us (13%)
  other arithmetic  69.8 us (10%)
    all_to_all x2, blocking collectives, body(): lax.all_to_all(as_sent(packed), ('ctx', 'dp'), split_axis=0, concat_axis=...  135 us
    all_to_all x4, waiting for transfers between devices, body(): lax.all_to_all(as_sent(packed), ('ctx', 'dp'), split_axis=0, concat_axis=...  59.5 us
    ppermute x16, starting transfers between devices, passed_along(): return lax.ppermute(array, axis, pairs)  43 us
    all_to_all x1, waiting for transfers between devices, body(): lax.all_to_all(back_q, ('ctx', 'dp'), split_axis=0, concat_axis=0, tiled=...  40.9 us
    gather x19, local copies, waits for them, and re-layouts, pack_rows(): member[picked]  38.1 us
    all_to_all x4, starting transfers between devices, body(): lax.all_to_all(as_sent(packed), ('ctx', 'dp'), split_axis=0, concat_axis=...  34.1 us
    add x8, other arithmetic, pass_step(): dquery_acc = dquery_acc + dquery_part  24 us
    ppermute x16, starting transfers between devices, shifted(): return lax.ppermute(value, axis, pairs)  22.2 us
  transfers between devices with their start and end apart: 38, of which 13 were waited for; matrix products, arithmetic and copies ran while one was open for 33% of the time, Pallas kernels for 0%

commit v1 on v0

v1 whole, which is shorter than its diff:
```python
import functools

import jax
import jax.numpy as jnp
from jax import lax
from jax.experimental import pallas as pl
from jax.experimental.pallas import tpu as pltpu
from jax.sharding import PartitionSpec as P

HDIM = 128
NZ = 8
ND = 8
PAIR = 88
SLOTS = ND * PAIR
QB = 128
FAST = 448
SLOW = 704
FAR = 1 << 20
LOG2E = 1.4426950408889634
MESH = pl.DeviceIdType.MESH
BF = jnp.bfloat16
F32 = jnp.float32
VMEM_SPEC = pl.BlockSpec(memory_space=pltpu.VMEM)
SMEM_SPEC = pl.BlockSpec(memory_space=pltpu.SMEM)
ANY_SPEC = pl.BlockSpec(memory_space=pl.ANY)


def dot(a, b):
    return jnp.dot(a, b, preferred_element_type=F32)


def one_hot_rows(count, row):
    ids = lax.broadcasted_iota(jnp.int32, (count, row.shape[1]), 0)
    return jnp.where(ids == row, 1.0, 0.0).astype(BF)


def one_hot_cols(col, count):
    ids = lax.broadcasted_iota(jnp.int32, (col.shape[0], count), 1)
    return jnp.where(ids == col, 1.0, 0.0).astype(BF)


def ends_of(x, axis):
    n = x.shape[axis]
    x = jnp.moveaxis(x, axis, -1)
    tri = jnp.arange(n)[:, None] >= jnp.arange(n)[None, :]
    out = jnp.sum(jnp.where(tri, x[..., None, :], 0), axis=-1)
    return jnp.moveaxis(out, -1, axis)


def steps_to(ids, ends, base):
    jump = base[..., 1:] - base[..., :-1]
    past = ends[..., None, :-1] <= ids[:, None]
    return ids + base[..., :1] + jnp.sum(jnp.where(past, jump[..., None, :], 0), axis=-1)


def source_slots(rc, tok):
    rank = lax.axis_index(("ctx", "dp"))
    flat = lax.dynamic_index_in_dim(rc, rank, 0, keepdims=False)
    n = flat.reshape(NZ, ND)
    ends = ends_of(flat, 0)
    within = ends_of(n, 0) - n + jnp.arange(ND, dtype=jnp.int32)[None, :] * PAIR
    base = within.reshape(-1) - (ends - flat)
    return steps_to(jnp.arange(tok, dtype=jnp.int32), ends, base)


def plane_counts(rc):
    d = lax.axis_index("dp")
    return lax.dynamic_index_in_dim(rc.reshape(NZ * ND, NZ, ND), d, 2, keepdims=False).reshape(NZ, ND, NZ)


def compact_index(q):
    c0 = lax.axis_index("ctx")
    m = lax.dynamic_index_in_dim(q, c0, 0, keepdims=False)
    rows_end = ends_of(m, 1)
    mt = m.T.reshape(-1)
    cs = (ends_of(mt, 0) - mt).reshape(NZ, ND).T
    ids = jnp.arange(PAIR, dtype=jnp.int32)
    idx = steps_to(ids, rows_end, cs - (rows_end - m))
    return jnp.where(ids[None, :] < rows_end[:, -1:], idx, -1).reshape(-1)


def positions(q, cap, tok):
    load = jnp.sum(q, axis=1)
    chunk = jnp.arange(NZ, dtype=jnp.int32)[None, :] * tok
    ends = ends_of(load, 1)
    base = chunk + (ends_of(load, 0) - load) - (ends - load)
    ids = jnp.arange(cap, dtype=jnp.int32)
    pos = steps_to(ids, ends, base)
    return jnp.where(ids[None, :] < ends[:, -1:], pos, FAR)


def pack_kernel(q_ref, k_ref, v_ref, o_ref, g_ref, l_ref, slot_ref, kv_ref, qg_ref, stat):
    tok, width = q_ref.shape
    heads = width // HDIM
    kvw = k_ref.shape[1]
    pick = one_hot_rows(SLOTS, slot_ref[...])
    kv_ref[:, :kvw] = dot(pick, k_ref[...]).astype(BF)
    kv_ref[:, kvw:] = dot(pick, v_ref[...]).astype(BF)
    stat[...] = jnp.zeros_like(stat)
    stat[:, :heads] = l_ref[...].astype(F32)
    for h in range(heads):
        at = slice(h * HDIM, (h + 1) * HDIM)
        both = g_ref[:, at].astype(F32) * o_ref[:, at].astype(F32)
        stat[:, heads + h:heads + h + 1] = jnp.sum(both, axis=1, keepdims=True)
    for h in range(0, heads, 2):
        at = slice(h * HDIM, (h + 2) * HDIM)
        qg_ref[:, at] = dot(pick, q_ref[:, at]).astype(BF)
        to = slice(width + h * HDIM, width + (h + 2) * HDIM)
        qg_ref[:, to] = dot(pick, g_ref[:, at]).astype(BF)
    qg_ref[:, 2 * width:] = dot(pick, stat[...].astype(BF)).astype(BF)


def pack(query, keys, values, output, grad_out, log_norm, slot_row):
    tok, width = query.shape
    kvw = 2 * keys.shape[1]
    qgw = 2 * width + HDIM
    return pl.pallas_call(
        pack_kernel,
        out_shape=(
            jax.ShapeDtypeStruct((SLOTS, kvw), BF),
            jax.ShapeDtypeStruct((SLOTS, qgw), BF),
        ),
        in_specs=[VMEM_SPEC] * 7,
        out_specs=(VMEM_SPEC, VMEM_SPEC),
        scratch_shapes=[pltpu.VMEM((tok, HDIM), F32)],
        compiler_params=pltpu.CompilerParams(vmem_limit_bytes=40 << 20),
        name="pack_rows",
    )(query, keys, values, output, grad_out, log_norm, slot_row)


def greet():
    z = lax.axis_index("ctx")
    d = lax.axis_index("dp")
    barrier = pltpu.get_barrier_semaphore()
    for s in range(1, ND):
        pl.semaphore_signal(barrier, inc=1, device_id={"dp": lax.rem(d + s, ND)}, device_id_type=MESH)
    for s in (1, NZ - 1):
        pl.semaphore_signal(barrier, inc=1, device_id={"ctx": lax.rem(z + s, NZ)}, device_id_type=MESH)
    pl.semaphore_wait(barrier, ND + 1)


def exchange(src, dst, send, recv):
    d = lax.axis_index("dp")
    copies = []
    for s in range(1, ND):
        to = lax.rem(d + s, ND)
        copies.append(pltpu.make_async_remote_copy(
            src_ref=src.at[to], dst_ref=dst.at[d], send_sem=send.at[s], recv_sem=recv.at[s],
            device_id={"dp": to}, device_id_type=MESH))
    return copies


def along(axis_by, src, dst, send, recv):
    z = lax.axis_index("ctx")
    return pltpu.make_async_remote_copy(
        src_ref=src, dst_ref=dst, send_sem=send, recv_sem=recv,
        device_id={"ctx": lax.rem(z + axis_by, NZ)}, device_id_type=MESH)


def dispatch_kernel(kv_ref, qg_ref, idx_ref, all_ref, rqg_ref, rkv, mine,
                    ks, kr, qs, qr, ls, fs, fr, bs, br):
    z = lax.axis_index("ctx")
    d = lax.axis_index("dp")
    cap = mine.shape[0]
    part = cap // 2
    greet()
    kv_copies = exchange(kv_ref, rkv, ks, kr)
    for c in kv_copies:
        c.start()
    own = pltpu.make_async_copy(kv_ref.at[d], rkv.at[d], ls.at[0])
    own.start()
    own.wait()
    for c in kv_copies:
        c.wait_recv()
    pick = one_hot_rows(cap, idx_ref[...])
    mine[...] = dot(pick, rkv[...].reshape(SLOTS, rkv.shape[2])).astype(BF)
    keep = pltpu.make_async_copy(mine, all_ref.at[z], ls.at[1])
    sent = []

    def hop(step, piece):
        rows = pl.ds(piece * part, part)
        for by, origin, send, recv, half in (
                (1, lax.rem(z - step + NZ, NZ), fs, fr, 0), (NZ - 1, lax.rem(z + step, NZ), bs, br, 1)):
            if step == NZ // 2 - 1 and piece != half:
                continue
            src = mine.at[rows] if step == 0 else all_ref.at[origin, rows]
            c = along(by, src, all_ref.at[origin, rows], send.at[step, piece], recv.at[step, piece])
            c.start()
            sent.append((step, piece, c))

    for piece in range(2):
        hop(0, piece)
    keep.start()
    qg_copies = exchange(qg_ref, rqg_ref, qs, qr)
    for c in qg_copies:
        c.start()
    own = pltpu.make_async_copy(qg_ref.at[d], rqg_ref.at[d], ls.at[2])
    own.start()
    for step in range(1, NZ // 2):
        for piece in range(2):
            for s, p, c in list(sent):
                if s == step - 1 and p == piece:
                    c.wait_recv()
            hop(step, piece)
    for s, p, c in sent:
        if s == NZ // 2 - 1:
            c.wait_recv()
    for s, p, c in sent:
        c.wait_send()
    for c in kv_copies:
        c.wait_send()
    for c in qg_copies:
        c.wait()
    keep.wait()
    own.wait()


def dispatch(kv, qg, idx_row, cap, cid):
    kvw = kv.shape[1]
    qgw = qg.shape[1]
    dma = pltpu.SemaphoreType.DMA
    return pl.pallas_call(
        dispatch_kernel,
        out_shape=(
            jax.ShapeDtypeStruct((NZ, cap, kvw), BF),
            jax.ShapeDtypeStruct((ND, PAIR, qgw), BF),
        ),
        in_specs=[VMEM_SPEC, ANY_SPEC, VMEM_SPEC],
        out_specs=(ANY_SPEC, ANY_SPEC),
        scratch_shapes=[
            pltpu.VMEM((ND, PAIR, kvw), BF), pltpu.VMEM((cap, kvw), BF),
            dma((ND,)), dma((ND,)), dma((ND,)), dma((ND,)), dma((3,)),
            dma((4, 2)), dma((4, 2)), dma((4, 2)), dma((4, 2)),
        ],
        compiler_params=pltpu.CompilerParams(
            collective_id=cid, has_side_effects=True, vmem_limit_bytes=40 << 20),
        name="dispatch_rows",
    )(kv.reshape(ND, PAIR, kvw), qg.reshape(ND, PAIR, qgw), idx_row)


def attend_kernel(group, kvh, kb, flag_ref, all_ref, rqg_ref, row_ref, col_ref, kpos_ref, qpos_ref,
                  dkv_ref, dq_ref, qs, gs, lse, dlt, dq, dkv):
    nq = qs.shape[1]
    capq = nq * QB
    width = group * kvh * HDIM
    heads = group * kvh
    kvw = kvh * HDIM
    scale = HDIM ** -0.5
    tiles = all_ref.shape[0] // kb
    pick = one_hot_rows(capq, row_ref[...])
    stat = lax.dot_general(rqg_ref[:, 2 * width:], pick, (((0,), (1,)), ((), ())), preferred_element_type=F32)
    for h in range(heads):
        g, r = divmod(h, group)
        for src, dst in ((0, qs), (width, gs)):
            part = dot(pick, rqg_ref[:, src + h * HDIM:src + (h + 1) * HDIM]).astype(BF)
            for i in range(nq):
                dst[g, i, r * QB:(r + 1) * QB, :] = part[i * QB:(i + 1) * QB, :]
        for i in range(nq):
            at = slice(i * QB, (i + 1) * QB)
            to = slice(r * QB, (r + 1) * QB)
            lse[g, i, :, to] = jnp.broadcast_to(stat[h:h + 1, at] * LOG2E, (8, QB))
            dlt[g, i, :, to] = jnp.broadcast_to(stat[heads + h:heads + h + 1, at], (8, QB))
    dq[...] = jnp.zeros_like(dq)
    dkv[...] = jnp.zeros_like(dkv)

    def q_block(i, _):
        hi = qpos_ref[i, 0:1, :]
        lo = qpos_ref[i, 1:2, :]

        def k_tile(t, _):
            @pl.when(flag_ref[i, t] != 0)
            def _():
                rows = pl.ds(pl.multiple_of(t * kb, 16), kb)
                kp = kpos_ref[rows, :]
                seen = (kp <= hi) & (kp >= lo)
                keep = jnp.where(seen, 1.0, 0.0)
                keep = jnp.concatenate([keep] * group, axis=1) > 0.5
                for g in range(kvh):
                    kt = all_ref[rows, g * HDIM:(g + 1) * HDIM]
                    vt = all_ref[rows, kvw + g * HDIM:kvw + (g + 1) * HDIM]
                    qt = qs[g, i]
                    gt = gs[g, i]
                    contract = (((1,), (1,)), ((), ()))
                    s = lax.dot_general(kt, qt, contract, preferred_element_type=F32)
                    p = jnp.where(keep, jnp.exp2(s * (scale * LOG2E) - lse[g, i, 0:1, :]), 0.0)
                    dp = lax.dot_general(vt, gt, contract, preferred_element_type=F32)
                    ds = (p * (dp - dlt[g, i, 0:1, :]) * scale).astype(BF)
                    dkv[rows, kvw + g * HDIM:kvw + (g + 1) * HDIM] += dot(p.astype(BF), gt)
                    dkv[rows, g * HDIM:(g + 1) * HDIM] += dot(ds, qt)
                    dq[g, i] += lax.dot_general(ds, kt, (((0,), (0,)), ((), ())), preferred_element_type=F32)
            return 0

        lax.fori_loop(0, tiles, k_tile, 0)
        return 0

    lax.fori_loop(0, nq, q_block, 0)
    dkv_ref[...] = dkv[...].astype(BF)
    back = one_hot_cols(col_ref[...], capq)
    for h in range(heads):
        g, r = divmod(h, group)
        rows = jnp.concatenate([dq[g, i, r * QB:(r + 1) * QB, :] for i in range(nq)], axis=0).astype(BF)
        dq_ref[:, h * HDIM:(h + 1) * HDIM] = dot(back, rows).astype(BF)


def attend(flags, kv_all, rqg, idx, kpos, qpos, group, kvh, kb):
    total, kvw = kv_all.shape
    nq = qpos.shape[0]
    width = group * kvh * HDIM
    return pl.pallas_call(
        functools.partial(attend_kernel, group, kvh, kb),
        out_shape=(
            jax.ShapeDtypeStruct((total, kvw), BF),
            jax.ShapeDtypeStruct((SLOTS, width), BF),
        ),
        in_specs=[SMEM_SPEC] + [VMEM_SPEC] * 6,
        out_specs=(VMEM_SPEC, VMEM_SPEC),
        scratch_shapes=[
            pltpu.VMEM((kvh, nq, group * QB, HDIM), BF), pltpu.VMEM((kvh, nq, group * QB, HDIM), BF),
            pltpu.VMEM((kvh, nq, 8, group * QB), F32), pltpu.VMEM((kvh, nq, 8, group * QB), F32),
            pltpu.VMEM((kvh, nq, group * QB, HDIM), F32), pltpu.VMEM((total, kvw), F32),
        ],
        compiler_params=pltpu.CompilerParams(vmem_limit_bytes=56 << 20),
        name="attention_grads",
    )(flags, kv_all, rqg, idx.reshape(1, -1), idx.reshape(-1, 1), kpos, qpos)


def return_kernel(dkv_ref, dq_ref, col_ref, rdq_ref, rdkv_ref, fin, bin_, fout, bout, slots,
                  qs, qr, ks, kr, ls, fs, fr, bs, br):
    z = lax.axis_index("ctx")
    d = lax.axis_index("dp")
    cap, kvw = dkv_ref.shape[1:]
    part = cap // 2
    last = NZ // 2 - 1
    greet()
    sent = []

    def hop(step, piece):
        rows = pl.ds(piece * part, part)
        for by, owner, send, recv, into, out, half in (
                (1, lax.rem(z + NZ // 2 - step, NZ), fs, fr, fin, fout, 0),
                (NZ - 1, lax.rem(z + NZ // 2 + step, NZ), bs, br, bin_, bout, 1)):
            if step == 0 and piece != half:
                continue
            if step == 0 or (step == 1 and piece != half):
                src = dkv_ref.at[owner, rows]
            else:
                for s, p, b, c in sent:
                    if s == step - 1 and p == piece and b == by:
                        c.wait_recv()
                out[step, rows, :] = (dkv_ref[owner, rows, :].astype(F32)
                                      + into[step - 1, rows, :].astype(F32)).astype(BF)
                src = out.at[step, rows]
            c = along(by, src, into.at[step, rows], send.at[step, piece], recv.at[step, piece])
            c.start()
            sent.append((step, piece, by, c))

    hop(0, 0)
    hop(0, 1)
    dq_copies = exchange(dq_ref, rdq_ref, qs, qr)
    for c in dq_copies:
        c.start()
    own = pltpu.make_async_copy(dq_ref.at[d], rdq_ref.at[d], ls.at[0])
    own.start()
    hop(1, 1)
    hop(1, 0)
    for step in range(2, NZ // 2):
        hop(step, 0)
        hop(step, 1)
    for s, p, b, c in sent:
        if s == last:
            c.wait_recv()
    total = (dkv_ref[z].astype(F32) + fin[last].astype(F32) + bin_[last].astype(F32)).astype(BF)
    back = one_hot_cols(col_ref[...], cap)
    slots[...] = dot(back, total).astype(BF).reshape(slots.shape)
    kv_copies = exchange(slots, rdkv_ref, ks, kr)
    for c in kv_copies:
        c.start()
    own_kv = pltpu.make_async_copy(slots.at[d], rdkv_ref.at[d], ls.at[1])
    own_kv.start()
    for s, p, b, c in sent:
        c.wait_send()
    own.wait()
    own_kv.wait()
    for c in dq_copies:
        c.wait()
    for c in kv_copies:
        c.wait()


def send_back(dkv, dq, idx, cid):
    total, kvw = dkv.shape
    cap = total // NZ
    width = dq.shape[1]
    dma = pltpu.SemaphoreType.DMA
    return pl.pallas_call(
        return_kernel,
        out_shape=(
            jax.ShapeDtypeStruct((ND, PAIR, width), BF),
            jax.ShapeDtypeStruct((ND, PAIR, kvw), BF),
        ),
        in_specs=[VMEM_SPEC, ANY_SPEC, VMEM_SPEC],
        out_specs=(ANY_SPEC, ANY_SPEC),
        scratch_shapes=[pltpu.VMEM((NZ // 2, cap, kvw), BF)] * 4 + [
            pltpu.VMEM((ND, PAIR, kvw), BF),
            dma((ND,)), dma((ND,)), dma((ND,)), dma((ND,)), dma((2,)),
            dma((4, 2)), dma((4, 2)), dma((4, 2)), dma((4, 2)),
        ],
        compiler_params=pltpu.CompilerParams(
            collective_id=cid, has_side_effects=True, vmem_limit_bytes=48 << 20),
        name="return_rows",
    )(dkv.reshape(NZ, cap, kvw), dq.reshape(ND, PAIR, width), idx.reshape(-1, 1))


def unpack_kernel(dq_ref, dkv_ref, slot_ref, gq_ref, gk_ref, gv_ref):
    width = dq_ref.shape[1]
    kvw = gk_ref.shape[1]
    pick = one_hot_cols(slot_ref[...], SLOTS)
    for at in range(0, width, 2 * HDIM):
        gq_ref[:, at:at + 2 * HDIM] = dot(pick, dq_ref[:, at:at + 2 * HDIM]).astype(BF)
    gk_ref[...] = dot(pick, dkv_ref[:, :kvw]).astype(BF)
    gv_ref[...] = dot(pick, dkv_ref[:, kvw:]).astype(BF)


def unpack(rdq, rdkv, slot_col):
    tok = slot_col.shape[0]
    width = rdq.shape[2]
    kvw = rdkv.shape[2] // 2
    return pl.pallas_call(
        unpack_kernel,
        out_shape=(
            jax.ShapeDtypeStruct((tok, width), BF),
            jax.ShapeDtypeStruct((tok, kvw), BF),
            jax.ShapeDtypeStruct((tok, kvw), BF),
        ),
        in_specs=[VMEM_SPEC] * 3,
        out_specs=(VMEM_SPEC,) * 3,
        compiler_params=pltpu.CompilerParams(vmem_limit_bytes=32 << 20),
        name="unpack_rows",
    )(rdq.reshape(SLOTS, width), rdkv.reshape(SLOTS, 2 * kvw), slot_col)


def body(query, keys, values, output, grad_out, log_norm, route_counts, doc_lengths):
    tok = query.shape[0]
    kvh = keys.shape[1] // HDIM
    group = query.shape[1] // keys.shape[1]
    slot = source_slots(route_counts, tok)
    q = plane_counts(route_counts)
    idx = compact_index(q)
    kv, qg = pack(query, keys, values, output, grad_out, log_norm, slot.reshape(1, -1))
    most = jnp.max(jnp.sum(route_counts.reshape(NZ, ND, NZ, ND), axis=(1, 2)))

    def run(cap, kb, cid, kv, qg):
        capq = -(-cap // QB) * QB
        pos = positions(q, cap, tok)
        mine = lax.dynamic_index_in_dim(pos, lax.axis_index("ctx"), 0, keepdims=False)
        mine = jnp.pad(mine, (0, capq - cap), constant_values=FAR)
        bounds = ends_of(doc_lengths[0], 0)
        lo = jnp.max(jnp.where(bounds[None, :] <= mine[:, None], bounds[None, :], 0), axis=1)
        hi = jnp.where(mine < FAR, mine, -1)
        qpos = jnp.stack([hi.reshape(-1, QB), lo.reshape(-1, QB)], axis=1)
        k_tiles = pos.reshape(-1, kb)
        k_min = jnp.min(k_tiles, axis=1)
        k_max = jnp.max(jnp.where(k_tiles < FAR, k_tiles, -1), axis=1)
        q_max = jnp.max(qpos[:, 0, :], axis=1)
        q_min = jnp.min(jnp.where(qpos[:, 0, :] >= 0, qpos[:, 1, :], FAR), axis=1)
        flags = ((k_min[None, :] <= q_max[:, None]) & (k_max[None, :] >= q_min[:, None])).astype(jnp.int32)
        kv_all, rqg = dispatch(kv, qg, idx.reshape(1, -1), cap, cid)
        dkv, dq = attend(flags, kv_all.reshape(NZ * cap, -1), rqg.reshape(SLOTS, -1), idx,
                         pos.reshape(-1, 1), qpos, group, kvh, kb)
        return send_back(dkv, dq, idx, cid + 1)

    rdq, rdkv = lax.cond(
        most <= FAST, functools.partial(run, FAST, 112, 0), functools.partial(run, SLOW, 176, 2), kv, qg)
    return unpack(rdq, rdkv, slot.reshape(-1, 1))


def solution(mesh):
    rows = P(("ctx", "dp"), "head")
    return jax.shard_map(
        body, mesh=mesh, in_specs=(rows,) * 6 + (P(), P("dp", None)), out_specs=(rows,) * 3, check_vma=False)
```

time: 674 us -> 225 us (0.33); the launches traced: 661 us -> 224 us
  Pallas kernels: 0 us -> 196 us
  blocking collectives: 157 us -> 0 us
  waiting for transfers between devices: 120 us -> 0 us
  starting transfers between devices: 114 us -> 0 us
  local copies, waits for them, and re-layouts: 114 us -> 21.3 us
  matrix products: 84.4 us -> 0 us
  other arithmetic: 69.8 us -> 4.72 us
    pallas_call x0 -> x5, Pallas kernels: none -> 196 us  [the longest x1 70.7 us: dispatch(): pl.pallas_call(dispatch_kernel, out_shape=(jax.ShapeDtypeStruct((NZ, cap,...]
    all_to_all x3 -> x0, blocking collectives: 157 us -> none  [the longest x2 135 us: body(): lax.all_to_all(as_sent(packed), ('ctx', 'dp'), split_axis=0, concat_axis=...]
    all_to_all x6 -> x0, waiting for transfers between devices: 106 us -> none  [the longest x4 59.5 us: body(): lax.all_to_all(as_sent(packed), ('ctx', 'dp'), split_axis=0, concat_axis=...]
    dot_general x40 -> x0, matrix products: 84.4 us -> none  [the longest x8 21.9 us: tile_grads(): jnp.einsum('qgrd,kgd->grqk', g_four, v_three, preferred_element_type=jnp....]
    ppermute x32 -> x0, starting transfers between devices: 65.2 us -> none  [the longest x16 43 us: passed_along(): return lax.ppermute(array, axis, pairs)]
    gather x28 -> x0, local copies, waits for them, and re-layouts: 59.6 us -> none  [the longest x19 38.1 us: pack_rows(): member[picked]]
    add x41 -> x3, other arithmetic: 52.4 us -> 0.26 us  [the longest x2 0.18 us: steps_to(): ids + base[..., :1]]
    all_to_all x6 -> x0, starting transfers between devices: 48.6 us -> none  [the longest x4 34.1 us: body(): lax.all_to_all(as_sent(packed), ('ctx', 'dp'), split_axis=0, concat_axis=...]
  transfers between devices with their start and end apart: 38 -> 0, of which waited for: 13 -> 0; matrix products, arithmetic and copies ran while one was open for 33% -> 0% of each run, Pallas kernels for 0% -> 0%
where the time goes in v1:
time: 225 us; the launch traced here: 224 us
  Pallas kernels  196 us (87%)
  local copies, waits for them, and re-layouts  21.3 us (9%)
  other arithmetic  4.72 us (2%)
    pallas_call x1, Pallas kernels, dispatch(): pl.pallas_call(dispatch_kernel, out_shape=(jax.ShapeDtypeStruct((NZ, cap,...  70.7 us
    pallas_call x1, Pallas kernels, send_back(): pl.pallas_call(return_kernel, out_shape=(jax.ShapeDtypeStruct((ND, PAIR,...  68.4 us
    pallas_call x1, Pallas kernels, attend(): pl.pallas_call(functools.partial(attend_kernel, group, kvh, kb), out_shap...  50.2 us
    cond x13, local copies, waits for them, and re-layouts  7.25 us
    unnamed x14, local copies, waits for them, and re-layouts  7.04 us

profile of v1, /device:TPU:4, one launch (start us, length us, event | category | flops | bytes accessed | tf_op | source)
XLA Modules:
  0.0 223.5 jit_solution(4328874265943783267)
XLA Ops:
  0.6 0.7 fusion.13
  1.5 0.8 copy.158
  3.6 0.8 copy.162.l_ref
  4.4 1.2 copy-done.9
  5.6 1.2 copy-done.10
  6.8 1.2 copy-done.11
  7.9 0.9 copy-done.12
  8.9 0.9 copy-done.13
  9.8 4.5 %pack_rows.1 = (bf16[704,512]{1,0:T(8,128)(2,1)S(1)}, bf16[704,2688]{1,0:T(8,128)(2,1)}) custom-call(bf16[352,1280]{1,0:T(8,128)(2,1)S(1)} %copy-done.9, bf16[352,256]{1,0:T(8,128)(2,1)S(1)} %copy-done.12, bf16[352,256]{1,0:T(8,128)(2,1)S(1)} %copy-done.13, bf16[352,1280]{1,0:T(8,128)(2,1)S(1)} %copy-done.10, bf16[352,1280]{1,0:T(8,128)(2,1)S(1)} %copy-done.11, ...), custom_call_target="tpu_custom_call" | custom-call | tf_op jit(solution)/shard_map/pack_rows/pallas_call | solution.py:117
  14.6 0.9 reshape.379
  15.6 0.6 reduce_max.67
  16.9 204.5 %conditional.1 = (bf16[704,1280]{1,0:T(8,128)(2,1)S(1)}, bf16[704,512]{1,0:T(8,128)(2,1)S(1)}) conditional(s32[]{:T(128)} %convert_element_type.9, (s32[8,8,8]{1,0,2:T(8,128)S(1)}, s32[1,4]{1,0:T(1,128)S(1)}, bf16[704,512]{1,0:T(8,128)(2,1)S(1)}, bf16[704,2688]{1,0:T(8,128)(2,1)}, s32[8,8]{1,0:T(8,128)S(1)}, /*index=5*/s32[8,88]{1,0:T(8,128)S(1)}, ...), branch_computations={%region_7.19_spmd, %region_19.31_spmd} | conditional | flops 218206 | bytes 51931440 | solution.py:472
  18.7 0.6 pad_add_fusion.1.qpos_ref
  20.1 0.7 and_convert_fusion.1.flag_ref
  20.7 2.8 %select_n.190.kpos_ref = s32[3584,1]{1,0:T(8,128)} reshape(s32[8,448]{1,0:T(8,128)S(1)} %add_select_fusion.3) | data formatting | bytes 28672 | tf_op jit(solution)/shard_map/cond/branch_1_fun/jit(_where)/select_n | solution.py:89
  24.0 70.7 %dispatch_rows.5 = (bf16[8,448,512]{2,1,0:T(8,128)(2,1)S(1)}, bf16[8,88,2688]{2,1,0:T(8,128)(2,1)S(1)}) custom-call(bf16[8,88,512]{2,1,0:T(8,128)(2,1)S(1)} %bitcast.107, bf16[8,88,2688]{2,1,0:T(8,128)(2,1)} %bitcast.104, s32[1,704]{1,0:T(1,128)S(1)} %reshape_reshape.10.idx_ref.row_ref), custom_call_target="tpu_custom_call" | custom-call | tf_op jit(solution)/shard_map/cond/branch_1_fun/dispatch_rows/pallas_call | solution.py:222
  94.7 1.8 copy-done.2
  96.5 1.8 copy-done.4
  98.4 0.9 reshape_reshape.17.col_ref
  99.3 50.2 %attention_grads.5 = (bf16[3584,512]{1,0:T(8,128)(2,1)}, bf16[704,1280]{1,0:T(8,128)(2,1)}) custom-call(s32[4,32]{1,0:T(4,128)} %and_convert_fusion.1.flag_ref, bf16[3584,512]{1,0:T(8,128)(2,1)} %bitcast.100, bf16[704,2688]{1,0:T(8,128)(2,1)} %bitcast.98, s32[1,704]{1,0:T(1,128)} %copy-done.15, s32[704,1]{1,0:T(8,128)} %reshape_reshape.17.col_ref, ...), custom_call_target="tpu_custom_call" | custom-call | tf_op jit(solution)/shard_map/cond/branch_1_fun/attention_grads/pallas_call | solution.py:309
  149.5 2.0 copy-done.3
  151.5 1.5 copy-done.7
  153.0 68.4 %return_rows.5 = (bf16[8,88,1280]{2,1,0:T(8,128)(2,1)S(1)}, bf16[8,88,512]{2,1,0:T(8,128)(2,1)S(1)}) custom-call(bf16[8,448,512]{2,1,0:T(8,128)(2,1)S(1)} %bitcast.99, bf16[8,88,1280]{2,1,0:T(8,128)(2,1)S(1)} %bitcast.101, s32[704,1]{1,0:T(8,128)S(1)} %copy-done.6), custom_call_target="tpu_custom_call" | custom-call | tf_op jit(solution)/shard_map/cond/branch_1_fun/return_rows/pallas_call | solution.py:395
  221.5 2.0 unpack_rows.1
  (72 shorter events, 4.6 us)
Async XLA Ops:
  0.6 16.2 %copy-start.16 = (s32[1,4]{1,0:T(1,128)S(1)}, s32[1,4]{1,0:T(1,128)}, u32[]{:S(2)}) copy-start(s32[1,4]{1,0:T(1,128)} %param.17) | copy-start | bytes 52
  4.4 1.2 copy-start.9
  5.6 1.2 copy-start.10
  6.8 1.2 copy-start.11
  7.9 0.9 copy-start.12
  8.9 0.9 copy-start.13
  24.0 75.3 %copy-start.15 = (s32[1,704]{1,0:T(1,128)}, s32[1,704]{1,0:T(1,128)S(1)}, u32[]{:S(2)}) copy-start(s32[1,704]{1,0:T(1,128)S(1)} %reshape_reshape.10.idx_ref.row_ref) | copy-start | bytes 8452 | tf_op jit(solution)/shard_map/cond
  94.7 1.8 copy-start.2
  96.5 1.8 copy-start.4
  99.3 50.2 %copy-start.6 = (s32[704,1]{1,0:T(8,128)S(1)}, s32[704,1]{1,0:T(8,128)}, u32[]{:S(2)}) copy-start(s32[704,1]{1,0:T(8,128)} %reshape_reshape.17.col_ref) | copy-start | bytes 8452 | tf_op jit(solution)/shard_map/cond
  149.5 2.0 copy-start.3
  151.5 1.5 copy-start.7

commit v2 on v1

v2 whole, which is shorter than its diff:
```python
import functools

import jax
import jax.numpy as jnp
from jax import lax
from jax.experimental import pallas as pl
from jax.experimental.pallas import tpu as pltpu
from jax.sharding import PartitionSpec as P

HDIM = 128
NZ = 8
ND = 8
QB = 128
KS = 32
FAST = (448, 80)
SLOW = (704, 88)
FAR = 1 << 20
LOG2E = 1.4426950408889634
MESH = pl.DeviceIdType.MESH
BF = jnp.bfloat16
F32 = jnp.float32
VMEM_SPEC = pl.BlockSpec(memory_space=pltpu.VMEM)
SMEM_SPEC = pl.BlockSpec(memory_space=pltpu.SMEM)
ANY_SPEC = pl.BlockSpec(memory_space=pl.ANY)


def dot(a, b):
    return jnp.dot(a, b, preferred_element_type=F32)


def one_hot_rows(count, row):
    ids = lax.broadcasted_iota(jnp.int32, (count, row.shape[1]), 0)
    return jnp.where(ids == row, 1.0, 0.0).astype(BF)


def dot_rows(a, b):
    return lax.dot_general(a, b, (((0,), (0,)), ((), ())), preferred_element_type=F32)


def ends_of(x, axis):
    n = x.shape[axis]
    x = jnp.moveaxis(x, axis, -1)
    tri = jnp.arange(n)[:, None] >= jnp.arange(n)[None, :]
    out = jnp.sum(jnp.where(tri, x[..., None, :], 0), axis=-1)
    return jnp.moveaxis(out, -1, axis)


def steps_to(ids, ends, base):
    jump = base[..., 1:] - base[..., :-1]
    past = ends[..., None, :-1] <= ids[:, None]
    return ids + base[..., :1] + jnp.sum(jnp.where(past, jump[..., None, :], 0), axis=-1)


def source_slots(rc, tok, pair):
    rank = lax.axis_index(("ctx", "dp"))
    flat = lax.dynamic_index_in_dim(rc, rank, 0, keepdims=False)
    n = flat.reshape(NZ, ND)
    ends = ends_of(flat, 0)
    within = ends_of(n, 0) - n + jnp.arange(ND, dtype=jnp.int32)[None, :] * pair
    base = within.reshape(-1) - (ends - flat)
    return steps_to(jnp.arange(tok, dtype=jnp.int32), ends, base)


def plane_counts(rc):
    d = lax.axis_index("dp")
    return lax.dynamic_index_in_dim(rc.reshape(NZ * ND, NZ, ND), d, 2, keepdims=False).reshape(NZ, ND, NZ)


def compact_index(q, pair):
    c0 = lax.axis_index("ctx")
    m = lax.dynamic_index_in_dim(q, c0, 0, keepdims=False)
    rows_end = ends_of(m, 1)
    mt = m.T.reshape(-1)
    cs = (ends_of(mt, 0) - mt).reshape(NZ, ND).T
    ids = jnp.arange(pair, dtype=jnp.int32)
    idx = steps_to(ids, rows_end, cs - (rows_end - m))
    return jnp.where(ids[None, :] < rows_end[:, -1:], idx, -1).reshape(-1)


def positions(q, cap, tok):
    load = jnp.sum(q, axis=1)
    chunk = jnp.arange(NZ, dtype=jnp.int32)[None, :] * tok
    ends = ends_of(load, 1)
    base = chunk + (ends_of(load, 0) - load) - (ends - load)
    ids = jnp.arange(cap, dtype=jnp.int32)
    pos = steps_to(ids, ends, base)
    return jnp.where(ids[None, :] < ends[:, -1:], pos, FAR), jnp.concatenate([ends, base], axis=1)


def greet():
    z = lax.axis_index("ctx")
    d = lax.axis_index("dp")
    barrier = pltpu.get_barrier_semaphore()
    for s in range(1, ND):
        pl.semaphore_signal(barrier, inc=1, device_id={"dp": lax.rem(d + s, ND)}, device_id_type=MESH)
    for s in (1, NZ - 1):
        pl.semaphore_signal(barrier, inc=1, device_id={"ctx": lax.rem(z + s, NZ)}, device_id_type=MESH)
    pl.semaphore_wait(barrier, ND + 1)


def exchange(src, dst, send, recv):
    d = lax.axis_index("dp")
    copies = []
    for s in range(1, ND):
        to = lax.rem(d + s, ND)
        copies.append(pltpu.make_async_remote_copy(
            src_ref=src.at[to], dst_ref=dst.at[d], send_sem=send.at[s], recv_sem=recv.at[s],
            device_id={"dp": to}, device_id_type=MESH))
    return copies


def along(axis_by, src, dst, send, recv):
    z = lax.axis_index("ctx")
    return pltpu.make_async_remote_copy(
        src_ref=src, dst_ref=dst, send_sem=send, recv_sem=recv,
        device_id={"ctx": lax.rem(z + axis_by, NZ)}, device_id_type=MESH)


def dispatch_kernel(q_ref, k_ref, v_ref, o_ref, g_ref, l_ref, slot_ref, idx_ref, all_ref, rq_ref, rg_ref,
                    qv, kvv, ov, gv, stat, skv, sq, sg, rkv, mine,
                    ins, ks, kr, qs, qr, gs, gr, ls, fs, fr, bs, br):
    z = lax.axis_index("ctx")
    d = lax.axis_index("dp")
    width = qv.shape[1]
    heads = width // HDIM
    kvw = k_ref.shape[1]
    slots, pair = skv.shape[0] * skv.shape[1], skv.shape[1]
    cap = mine.shape[0]
    part = cap // 2
    loads = []
    for n, (src, dst) in enumerate(((k_ref, kvv.at[:, :kvw]), (v_ref, kvv.at[:, kvw:]),
                                    (q_ref, qv), (g_ref, gv), (o_ref, ov))):
        c = pltpu.make_async_copy(src, dst, ins.at[n])
        c.start()
        loads.append(c)
    greet()
    pick = one_hot_rows(slots, slot_ref[...])
    loads[0].wait()
    loads[1].wait()
    skv[...] = dot(pick, kvv[...]).astype(BF).reshape(skv.shape)
    kv_copies = exchange(skv, rkv, ks, kr)
    for c in kv_copies:
        c.start()
    own = [pltpu.make_async_copy(skv.at[d], rkv.at[d], ls.at[0])]
    own[0].start()
    loads[2].wait()
    for at in range(0, width, 2 * HDIM):
        at = slice(at, at + 2 * HDIM)
        sq[:, :, at] = dot(pick, qv[:, at]).astype(BF).reshape(ND, pair, 2 * HDIM)
    q_copies = exchange(sq, rq_ref, qs, qr)
    for c in q_copies:
        c.start()
    own.append(pltpu.make_async_copy(sq.at[d], rq_ref.at[d], ls.at[1]))
    own[1].start()
    loads[3].wait()
    loads[4].wait()
    stat[...] = jnp.zeros_like(stat)
    for h in range(heads):
        at = slice(h * HDIM, (h + 1) * HDIM)
        both = gv[:, at].astype(F32) * ov[:, at].astype(F32)
        stat[:, h:h + 1] = jnp.sum(both, axis=1, keepdims=True)
    for at in range(0, width, 2 * HDIM):
        at = slice(at, at + 2 * HDIM)
        sg[:, :, at] = dot(pick, gv[:, at]).astype(BF).reshape(ND, pair, 2 * HDIM)
    sg[:, :, width:] = dot(pick, stat[...].astype(BF)).astype(BF).reshape(ND, pair, HDIM)
    lse = lax.dot_general(pick, l_ref[...], (((1,), (1,)), ((), ())), preferred_element_type=F32)
    sg[:, :, width + heads:width + 2 * heads] = lse.astype(BF).reshape(ND, pair, heads)
    g_copies = exchange(sg, rg_ref, gs, gr)
    for c in g_copies:
        c.start()
    own.append(pltpu.make_async_copy(sg.at[d], rg_ref.at[d], ls.at[2]))
    own[2].start()
    own[0].wait()
    for c in kv_copies:
        c.wait_recv()
    mine[...] = dot(one_hot_rows(cap, idx_ref[...]), rkv[...].reshape(slots, 2 * kvw)).astype(BF)
    sent = []

    def hop(step, piece):
        rows = pl.ds(piece * part, part)
        for by, origin, send, recv, half in (
                (1, lax.rem(z - step + NZ, NZ), fs, fr, 0), (NZ - 1, lax.rem(z + step, NZ), bs, br, 1)):
            if step == NZ // 2 - 1 and piece != half:
                continue
            src = mine.at[rows] if step == 0 else all_ref.at[origin, rows]
            c = along(by, src, all_ref.at[origin, rows], send.at[step, piece], recv.at[step, piece])
            c.start()
            sent.append((step, piece, c))

    for piece in range(2):
        hop(0, piece)
    own.append(pltpu.make_async_copy(mine, all_ref.at[z], ls.at[3]))
    own[3].start()
    for step in range(1, NZ // 2):
        for piece in range(2):
            for s, p, c in list(sent):
                if s == step - 1 and p == piece:
                    c.wait_recv()
            hop(step, piece)
    for s, p, c in sent:
        if s == NZ // 2 - 1:
            c.wait_recv()
        c.wait_send()
    for c in kv_copies:
        c.wait_send()
    for c in q_copies + g_copies:
        c.wait()
    for c in own[1:]:
        c.wait()


def dispatch(query, keys, values, output, grad_out, log_norm, slot_row, idx_row, cap, pair, cid):
    tok, width = query.shape
    kvw = 2 * keys.shape[1]
    gw = width + HDIM
    dma = pltpu.SemaphoreType.DMA
    return pl.pallas_call(
        dispatch_kernel,
        out_shape=(
            jax.ShapeDtypeStruct((NZ, cap, kvw), BF),
            jax.ShapeDtypeStruct((ND, pair, width), BF),
            jax.ShapeDtypeStruct((ND, pair, gw), BF),
        ),
        in_specs=[ANY_SPEC] * 5 + [VMEM_SPEC] * 3,
        out_specs=(ANY_SPEC,) * 3,
        scratch_shapes=[
            pltpu.VMEM((tok, width), BF), pltpu.VMEM((tok, kvw), BF),
            pltpu.VMEM((tok, width), BF), pltpu.VMEM((tok, width), BF), pltpu.VMEM((tok, HDIM), F32),
            pltpu.VMEM((ND, pair, kvw), BF), pltpu.VMEM((ND, pair, width), BF), pltpu.VMEM((ND, pair, gw), BF),
            pltpu.VMEM((ND, pair, kvw), BF), pltpu.VMEM((cap, kvw), BF),
            dma((5,)), dma((ND,)), dma((ND,)), dma((ND,)), dma((ND,)), dma((ND,)), dma((ND,)), dma((4,)),
            dma((4, 2)), dma((4, 2)), dma((4, 2)), dma((4, 2)),
        ],
        compiler_params=pltpu.CompilerParams(
            collective_id=cid, has_side_effects=True, vmem_limit_bytes=56 << 20),
        name="dispatch_rows",
    )(query, keys, values, output, grad_out, log_norm.T, slot_row, idx_row)


def attend_kernel(group, kvh, span_ref, tab_ref, all_hbm, rq_hbm, rg_hbm, row_ref, qpos_ref, dkv_ref, dq_ref,
                  all_ref, rq_ref, rg_ref, qs, gs, lse, dlt, dq, dkv, kpos, ins):
    nq = qs.shape[1]
    capq = nq * QB
    heads = group * kvh
    width = heads * HDIM
    kvw = kvh * HDIM
    scale = HDIM ** -0.5
    cap = all_ref.shape[1]
    tile = NZ * KS
    loads = []
    for n, (src, dst) in enumerate(((rq_hbm, rq_ref), (rg_hbm, rg_ref), (all_hbm, all_ref))):
        c = pltpu.make_async_copy(src, dst, ins.at[n])
        c.start()
        loads.append(c)
    pick = one_hot_rows(capq, row_ref[...])
    ids = lax.broadcasted_iota(jnp.int32, (cap, HDIM), 0)
    for z in range(NZ):
        p = ids + tab_ref[z, NZ]
        for c in range(NZ):
            jump = tab_ref[z, NZ + c + 1] - tab_ref[z, NZ + c] if c + 1 < NZ else FAR
            p = p + jnp.where(ids >= tab_ref[z, c], jump, 0)
        kpos[z] = p
    dq[...] = jnp.zeros_like(dq)
    dkv[...] = jnp.zeros_like(dkv)
    for load, src, dst in ((loads[0], rq_ref, qs), (loads[1], rg_ref, gs)):
        load.wait()
        for h in range(0, heads, 2):
            both = dot(pick, src[:, h * HDIM:(h + 2) * HDIM]).astype(BF)
            for e in range(2):
                g, r = divmod(h + e, group)
                for i in range(nq):
                    dst[g, i, r * QB:(r + 1) * QB, :] = both[i * QB:(i + 1) * QB, e * HDIM:(e + 1) * HDIM]
    stat = lax.dot_general(rg_ref[:, width:], pick, (((0,), (1,)), ((), ())), preferred_element_type=F32)
    for h in range(heads):
        g, r = divmod(h, group)
        for i in range(nq):
            at = slice(i * QB, (i + 1) * QB)
            to = slice(r * QB, (r + 1) * QB)
            dlt[g, i, :, to] = jnp.broadcast_to(stat[h:h + 1, at], (8, QB))
            lse[g, i, :, to] = jnp.broadcast_to(stat[heads + h:heads + h + 1, at] * LOG2E, (8, QB))
    loads[2].wait()

    def q_block(i, _):
        hi = qpos_ref[i, 0:1, :]
        lo = qpos_ref[i, 1:2, :]

        def k_tile(t, _):
            rows = pl.ds(pl.multiple_of(t * KS, KS), KS)
            kp = kpos[:, rows, :].reshape(tile, HDIM)
            keep = jnp.where((kp <= hi) & (kp >= lo), 1.0, 0.0)
            keep = jnp.concatenate([keep] * group, axis=1) > 0.5
            for g in range(kvh):
                kc = slice(g * HDIM, (g + 1) * HDIM)
                vc = slice(kvw + g * HDIM, kvw + (g + 1) * HDIM)
                kt = all_ref[:, rows, kc].reshape(tile, HDIM)
                vt = all_ref[:, rows, vc].reshape(tile, HDIM)
                qt = qs[g, i]
                gt = gs[g, i]
                last = (((1,), (1,)), ((), ()))
                s = lax.dot_general(kt, qt, last, preferred_element_type=F32)
                p = jnp.where(keep, jnp.exp2(s * (scale * LOG2E) - lse[g, i, 0:1, :]), 0.0)
                dp = lax.dot_general(vt, gt, last, preferred_element_type=F32)
                ds = (p * (dp - dlt[g, i, 0:1, :]) * scale).astype(BF)
                dkv[:, rows, vc] += dot(p.astype(BF), gt).reshape(NZ, KS, HDIM)
                dkv[:, rows, kc] += dot(ds, qt).reshape(NZ, KS, HDIM)
                dq[g, i] += dot_rows(ds, kt)
            return 0

        lax.fori_loop(span_ref[0, i], span_ref[1, i], k_tile, 0)
        return 0

    lax.fori_loop(0, nq, q_block, 0)
    dkv_ref[...] = dkv[...].astype(BF)
    for h in range(0, heads, 2):
        cols = []
        for e in range(2):
            g, r = divmod(h + e, group)
            cols.append(jnp.concatenate([dq[g, i, r * QB:(r + 1) * QB, :] for i in range(nq)], axis=0).astype(BF))
        dq_ref[:, h * HDIM:(h + 2) * HDIM] = dot_rows(pick, jnp.concatenate(cols, axis=1)).astype(BF)


def attend(span, tab, kv_all, rq, rg, idx_row, qpos, group, kvh):
    cap, kvw = kv_all.shape[1:]
    nq = qpos.shape[0]
    slots, width = rq.shape
    return pl.pallas_call(
        functools.partial(attend_kernel, group, kvh),
        out_shape=(
            jax.ShapeDtypeStruct((NZ, cap, kvw), BF),
            jax.ShapeDtypeStruct((slots, width), BF),
        ),
        in_specs=[SMEM_SPEC] * 2 + [ANY_SPEC] * 3 + [VMEM_SPEC] * 2,
        out_specs=(VMEM_SPEC, VMEM_SPEC),
        scratch_shapes=[
            pltpu.VMEM((NZ, cap, kvw), BF), pltpu.VMEM(rq.shape, BF), pltpu.VMEM(rg.shape, BF),
            pltpu.VMEM((kvh, nq, group * QB, HDIM), BF), pltpu.VMEM((kvh, nq, group * QB, HDIM), BF),
            pltpu.VMEM((kvh, nq, 8, group * QB), F32), pltpu.VMEM((kvh, nq, 8, group * QB), F32),
            pltpu.VMEM((kvh, nq, group * QB, HDIM), F32), pltpu.VMEM((NZ, cap, kvw), F32),
            pltpu.VMEM((NZ, cap, HDIM), jnp.int32),
            pltpu.SemaphoreType.DMA((3,)),
        ],
        compiler_params=pltpu.CompilerParams(vmem_limit_bytes=60 << 20),
        name="attention_grads",
    )(span, tab, kv_all, rq, rg, idx_row, qpos)


def return_kernel(dkv_hbm, dq_ref, idx_ref, rdq_ref, rdkv_ref, dkv_ref, fin, bin_, fout, bout, slots,
                  qs, qr, ks, kr, ls, fs, fr, bs, br):
    z = lax.axis_index("ctx")
    d = lax.axis_index("dp")
    cap, kvw = dkv_ref.shape[1:]
    part = cap // 2
    last = NZ // 2 - 1
    load = pltpu.make_async_copy(dkv_hbm, dkv_ref, ls.at[2])
    load.start()
    greet()
    sent = []

    def hop(step, piece):
        rows = pl.ds(piece * part, part)
        for by, owner, send, recv, into, out, half in (
                (1, lax.rem(z + NZ // 2 - step, NZ), fs, fr, fin, fout, 0),
                (NZ - 1, lax.rem(z + NZ // 2 + step, NZ), bs, br, bin_, bout, 1)):
            if step == 0 and piece != half:
                continue
            if step == 0 or (step == 1 and piece != half):
                src = dkv_hbm.at[owner, rows]
            else:
                for s, p, b, c in sent:
                    if s == step - 1 and p == piece and b == by:
                        c.wait_recv()
                out[step, rows, :] = (dkv_ref[owner, rows, :].astype(F32)
                                      + into[step - 1, rows, :].astype(F32)).astype(BF)
                src = out.at[step, rows]
            c = along(by, src, into.at[step, rows], send.at[step, piece], recv.at[step, piece])
            c.start()
            sent.append((step, piece, by, c))

    hop(0, 0)
    hop(0, 1)
    dq_copies = exchange(dq_ref, rdq_ref, qs, qr)
    for c in dq_copies:
        c.start()
    own = pltpu.make_async_copy(dq_ref.at[d], rdq_ref.at[d], ls.at[0])
    own.start()
    load.wait()
    for step in range(1, NZ // 2):
        hop(step, 0)
        hop(step, 1)
    for s, p, b, c in sent:
        if s == last:
            c.wait_recv()
    total = (dkv_ref[z].astype(F32) + fin[last].astype(F32) + bin_[last].astype(F32)).astype(BF)
    slots[...] = dot_rows(one_hot_rows(cap, idx_ref[...]), total).astype(BF).reshape(slots.shape)
    kv_copies = exchange(slots, rdkv_ref, ks, kr)
    for c in kv_copies:
        c.start()
    own_kv = pltpu.make_async_copy(slots.at[d], rdkv_ref.at[d], ls.at[1])
    own_kv.start()
    for s, p, b, c in sent:
        c.wait_send()
    own.wait()
    own_kv.wait()
    for c in dq_copies:
        c.wait()
    for c in kv_copies:
        c.wait()


def send_back(dkv, dq, idx_row, cid):
    cap, kvw = dkv.shape[1:]
    pair, width = dq.shape[1:]
    dma = pltpu.SemaphoreType.DMA
    return pl.pallas_call(
        return_kernel,
        out_shape=(
            jax.ShapeDtypeStruct((ND, pair, width), BF),
            jax.ShapeDtypeStruct((ND, pair, kvw), BF),
        ),
        in_specs=[ANY_SPEC, ANY_SPEC, VMEM_SPEC],
        out_specs=(ANY_SPEC, ANY_SPEC),
        scratch_shapes=[pltpu.VMEM((NZ, cap, kvw), BF)] + [pltpu.VMEM((NZ // 2, cap, kvw), BF)] * 4 + [
            pltpu.VMEM((ND, pair, kvw), BF),
            dma((ND,)), dma((ND,)), dma((ND,)), dma((ND,)), dma((3,)),
            dma((4, 2)), dma((4, 2)), dma((4, 2)), dma((4, 2)),
        ],
        compiler_params=pltpu.CompilerParams(
            collective_id=cid, has_side_effects=True, vmem_limit_bytes=56 << 20),
        name="return_rows",
    )(dkv, dq, idx_row)


def unpack_kernel(dq_ref, dkv_ref, slot_ref, gq_ref, gk_ref, gv_ref):
    slots, width = dq_ref.shape
    kvw = gk_ref.shape[1]
    pick = one_hot_rows(slots, slot_ref[...])
    for at in range(0, width, 2 * HDIM):
        gq_ref[:, at:at + 2 * HDIM] = dot_rows(pick, dq_ref[:, at:at + 2 * HDIM]).astype(BF)
    gk_ref[...] = dot_rows(pick, dkv_ref[:, :kvw]).astype(BF)
    gv_ref[...] = dot_rows(pick, dkv_ref[:, kvw:]).astype(BF)


def unpack(rdq, rdkv, slot_row):
    tok = slot_row.shape[1]
    slots = rdq.shape[0] * rdq.shape[1]
    width = rdq.shape[2]
    kvw = rdkv.shape[2] // 2
    return pl.pallas_call(
        unpack_kernel,
        out_shape=(
            jax.ShapeDtypeStruct((tok, width), BF),
            jax.ShapeDtypeStruct((tok, kvw), BF),
            jax.ShapeDtypeStruct((tok, kvw), BF),
        ),
        in_specs=[VMEM_SPEC] * 3,
        out_specs=(VMEM_SPEC,) * 3,
        compiler_params=pltpu.CompilerParams(vmem_limit_bytes=32 << 20),
        name="unpack_rows",
    )(rdq.reshape(slots, width), rdkv.reshape(slots, 2 * kvw), slot_row)


def body(query, keys, values, output, grad_out, log_norm, route_counts, doc_lengths):
    tok = query.shape[0]
    kvh = keys.shape[1] // HDIM
    group = query.shape[1] // keys.shape[1]
    loads = jnp.sum(route_counts.reshape(NZ, ND, NZ, ND), axis=2)
    fits = (jnp.max(jnp.sum(loads, axis=1)) <= FAST[0]) & (jnp.max(loads) <= FAST[1])

    def run(size, cid, *rows):
        cap, pair = size
        capq = -(-cap // QB) * QB
        q = plane_counts(route_counts)
        slot = source_slots(route_counts, tok, pair).reshape(1, -1)
        idx = compact_index(q, pair).reshape(1, -1)
        pos, tab = positions(q, cap, tok)
        mine = lax.dynamic_index_in_dim(pos, lax.axis_index("ctx"), 0, keepdims=False)
        mine = jnp.pad(mine, (0, capq - cap), constant_values=FAR)
        bounds = ends_of(doc_lengths[0], 0)
        lo = jnp.max(jnp.where(bounds[None, :] <= mine[:, None], bounds[None, :], 0), axis=1)
        hi = jnp.where(mine < FAR, mine, -1)
        qpos = jnp.stack([hi.reshape(-1, QB), lo.reshape(-1, QB)], axis=1)
        k_tiles = pos.reshape(NZ, -1, KS)
        k_min = jnp.min(k_tiles, axis=(0, 2))
        k_max = jnp.max(k_tiles, axis=(0, 2))
        q_max = jnp.max(qpos[:, 0, :], axis=1)
        q_min = jnp.min(jnp.where(qpos[:, 0, :] >= 0, qpos[:, 1, :], FAR), axis=1)
        span = jnp.stack([
            jnp.sum((k_max[None, :] < q_min[:, None]).astype(jnp.int32), axis=1),
            jnp.sum((k_min[None, :] <= q_max[:, None]).astype(jnp.int32), axis=1)])
        kv_all, rq, rg = dispatch(*rows, slot, idx, cap, pair, cid)
        slots = ND * pair
        dkv, dq = attend(span, tab, kv_all, rq.reshape(slots, -1), rg.reshape(slots, -1), idx, qpos, group, kvh)
        rdq, rdkv = send_back(dkv, dq.reshape(ND, pair, -1), idx, cid + 1)
        return unpack(rdq, rdkv, slot)

    return lax.cond(fits, functools.partial(run, FAST, 0), functools.partial(run, SLOW, 2),
                    query, keys, values, output, grad_out, log_norm)


def solution(mesh):
    rows = P(("ctx", "dp"), "head")
    return jax.shard_map(
        body, mesh=mesh, in_specs=(rows,) * 6 + (P(), P("dp", None)), out_specs=(rows,) * 3, check_vma=False)
```

time: 225 us -> 174 us (0.77)
  Pallas kernels: 196 us -> 154 us
  local copies, waits for them, and re-layouts: 21.3 us -> 8.17 us
  other arithmetic: 4.72 us -> 8.37 us
    pallas_call x3 -> x2, Pallas kernels: 123 us -> 87.3 us  [the longest x1 54 us: send_back(): pl.pallas_call(return_kernel, out_shape=(jax.ShapeDtypeStruct((ND, pair,...]
    unnamed x14 -> x0, local copies, waits for them, and re-layouts: 7.04 us -> none
    pallas_call x1, Pallas kernels: 70.7 us -> 65.1 us  [dispatch(): pl.pallas_call(dispatch_kernel, out_shape=(jax.ShapeDtypeStruct((NZ, cap,...]
    cond x13 -> x6, local copies, waits for them, and re-layouts: 7.25 us -> 2.51 us
where the time goes in v2:
time: 174 us; the launch traced here: 173 us
  Pallas kernels  154 us (89%)
  other arithmetic  8.37 us (5%)
  local copies, waits for them, and re-layouts  8.17 us (5%)
  between operations  1.96 us (1%)
    pallas_call x1, Pallas kernels, dispatch(): pl.pallas_call(dispatch_kernel, out_shape=(jax.ShapeDtypeStruct((NZ, cap,...  65.1 us
    pallas_call x1, Pallas kernels, send_back(): pl.pallas_call(return_kernel, out_shape=(jax.ShapeDtypeStruct((ND, pair,...  54 us
    pallas_call x1, Pallas kernels, attend(): pl.pallas_call(functools.partial(attend_kernel, group, kvh), out_shape=(j...  33.3 us

profile of v2, /device:TPU:4, one launch (start us, length us, event | category | flops | bytes accessed | tf_op | source)
XLA Modules:
  0.0 173.2 jit_solution(11842912627552655444)
XLA Ops:
  0.6 0.9 reshape.379
  1.6 0.6 reduce_max.86
  2.9 0.6 reduce_max.87
  4.2 169.0 %conditional.1 = ((bf16[352,1280]{1,0:T(8,128)(2,1)}, bf16[352,256]{1,0:T(8,128)(2,1)}, bf16[352,256]{1,0:T(8,128)(2,1)})) conditional(s32[]{:T(128)} %convert_element_type.15, (s32[64,64]{1,0:T(8,128)}, s32[1,4]{1,0:T(1,128)}, bf16[352,10]{0,1:T(8,128)(2,1)}, bf16[352,1280]{1,0:T(8,128)(2,1)}, bf16[352,256]{1,0:T(8,128)(2,1)}, ...), branch_computations={%region_4.25_spmd, %region_25.46_spmd} | conditional | flops 281179 | bytes 10311290 | solution.py:496
  4.4 0.8 select_reduce_fusion.21
  5.3 0.8 copy.94
  6.8 0.2 reduce_sum.243
  7.5 0.6 select_reduce_fusion.14
  8.6 0.6 dynamic-slice.2
  9.6 0.6 reshape_add_fusion.1.slot_ref
  10.2 0.2 slice_reduce_fusion.5
  10.4 0.6 dynamic-slice.3
  11.0 0.7 pad_add_fusion.3.tab_ref
  12.1 0.7 select_n.162.idx_ref.row_ref
  12.9 1.2 compare_select_fusion.2
  14.4 0.6 pad_add_fusion.4.qpos_ref
  15.2 0.2 convert_reduce_fusion.3
  15.8 0.5 pad_add_fusion.5.span_ref
  16.3 65.1 %dispatch_rows.3 = (bf16[8,448,512]{2,1,0:T(8,128)(2,1)}, bf16[8,80,1280]{2,1,0:T(8,128)(2,1)}, bf16[8,80,1408]{2,1,0:T(8,128)(2,1)}) custom-call(bf16[352,1280]{1,0:T(8,128)(2,1)} %get-tuple-element.49.q_ref, bf16[352,256]{1,0:T(8,128)(2,1)} %get-tuple-element.50.k_ref, bf16[352,256]{1,0:T(8,128)(2,1)} %get-tuple-element.51.v_ref, ...), custom_call_target="tpu_custom_call" | custom-call | tf_op jit(solution)/shard_map/cond/branch_1_fun/dispatch_rows/pallas_call | solution.py:217
  81.4 33.3 %attention_grads.3 = (bf16[8,448,512]{2,1,0:T(8,128)(2,1)}, bf16[640,1280]{1,0:T(8,128)(2,1)}) custom-call(s32[2,4]{1,0:T(2,128)} %pad_add_fusion.5.span_ref, s32[8,16]{1,0:T(8,128)} %pad_add_fusion.3.tab_ref, bf16[8,448,512]{2,1,0:T(8,128)(2,1)} %get-tuple-element.55.all_hbm, bf16[640,1280]{1,0:T(8,128)(2,1)} %bitcast.120, bf16[640,1408]{1,0:T(8,128)(2,1)} %bitcast.117, ...), custom_call_target="tpu_custom_call" | custom-call | tf_op jit(solution)/shard_map/cond/branch_1_fun/attention_grads/pallas_call | solution.py:326
  114.7 54.0 %return_rows.3 = (bf16[8,80,1280]{2,1,0:T(8,128)(2,1)}, bf16[8,80,512]{2,1,0:T(8,128)(2,1)}) custom-call(bf16[8,448,512]{2,1,0:T(8,128)(2,1)} %get-tuple-element.58.dkv_hbm, bf16[8,80,1280]{2,1,0:T(8,128)(2,1)} %bitcast.119, s32[1,640]{1,0:T(1,128)} %select_n.162.idx_ref.row_ref), custom_call_target="tpu_custom_call" | custom-call | tf_op jit(solution)/shard_map/cond/branch_1_fun/return_rows/pallas_call | solution.py:414
  168.7 1.4 copy-done.1
  170.2 1.1 copy-done.3
  171.2 2.0 %unpack_rows.3 = (bf16[352,1280]{1,0:T(8,128)(2,1)}, bf16[352,256]{1,0:T(8,128)(2,1)}, bf16[352,256]{1,0:T(8,128)(2,1)}) custom-call(bf16[640,1280]{1,0:T(8,128)(2,1)S(1)} %bitcast.112, bf16[640,512]{1,0:T(8,128)(2,1)S(1)} %bitcast.114, s32[1,352]{1,0:T(1,128)S(1)} %copy-done.5), custom_call_target="tpu_custom_call" | custom-call | tf_op jit(solution)/shard_map/cond/branch_1_fun/unpack_rows/pallas_call | solution.py:448
  (52 shorter events, 3.6 us)
Async XLA Ops:
  114.7 54.0 %copy-start.5 = (s32[1,352]{1,0:T(1,128)S(1)}, s32[1,352]{1,0:T(1,128)}, u32[]{:S(2)}) copy-start(s32[1,352]{1,0:T(1,128)} %reshape_add_fusion.1.slot_ref) | copy-start | bytes 4228 | tf_op jit(solution)/shard_map/cond
  168.7 1.4 copy-start.1
  170.2 1.1 copy-start.3

commit v3 on v2

--- a/solution.py
+++ b/solution.py
@@ -37,54 +37,102 @@
     return lax.dot_general(a, b, (((0,), (0,)), ((), ())), preferred_element_type=F32)
 
 
-def ends_of(x, axis):
-    n = x.shape[axis]
-    x = jnp.moveaxis(x, axis, -1)
-    tri = jnp.arange(n)[:, None] >= jnp.arange(n)[None, :]
-    out = jnp.sum(jnp.where(tri, x[..., None, :], 0), axis=-1)
-    return jnp.moveaxis(out, -1, axis)
-
-
-def steps_to(ids, ends, base):
-    jump = base[..., 1:] - base[..., :-1]
-    past = ends[..., None, :-1] <= ids[:, None]
-    return ids + base[..., :1] + jnp.sum(jnp.where(past, jump[..., None, :], 0), axis=-1)
-
-
-def source_slots(rc, tok, pair):
-    rank = lax.axis_index(("ctx", "dp"))
-    flat = lax.dynamic_index_in_dim(rc, rank, 0, keepdims=False)
-    n = flat.reshape(NZ, ND)
-    ends = ends_of(flat, 0)
-    within = ends_of(n, 0) - n + jnp.arange(ND, dtype=jnp.int32)[None, :] * pair
-    base = within.reshape(-1) - (ends - flat)
-    return steps_to(jnp.arange(tok, dtype=jnp.int32), ends, base)
-
-
-def plane_counts(rc):
+def tables_kernel(tok, rc_ref, counts_ref, doc_ref, slot_ref, idx_ref, qpos_ref, tab_ref, span_ref, fits_ref, tops):
+    z = lax.axis_index("ctx")
     d = lax.axis_index("dp")
-    return lax.dynamic_index_in_dim(rc.reshape(NZ * ND, NZ, ND), d, 2, keepdims=False).reshape(NZ, ND, NZ)
-
-
-def compact_index(q, pair):
-    c0 = lax.axis_index("ctx")
-    m = lax.dynamic_index_in_dim(q, c0, 0, keepdims=False)
-    rows_end = ends_of(m, 1)
-    mt = m.T.reshape(-1)
-    cs = (ends_of(mt, 0) - mt).reshape(NZ, ND).T
-    ids = jnp.arange(pair, dtype=jnp.int32)
-    idx = steps_to(ids, rows_end, cs - (rows_end - m))
-    return jnp.where(ids[None, :] < rows_end[:, -1:], idx, -1).reshape(-1)
-
-
-def positions(q, cap, tok):
-    load = jnp.sum(q, axis=1)
-    chunk = jnp.arange(NZ, dtype=jnp.int32)[None, :] * tok
-    ends = ends_of(load, 1)
-    base = chunk + (ends_of(load, 0) - load) - (ends - load)
-    ids = jnp.arange(cap, dtype=jnp.int32)
-    pos = steps_to(ids, ends, base)
-    return jnp.where(ids[None, :] < ends[:, -1:], pos, FAR), jnp.concatenate([ends, base], axis=1)
+    owners = NZ * ND
+    part_of = lax.broadcasted_iota(jnp.int32, (owners, HDIM), 0) % ND
+    lanes = lax.broadcasted_iota(jnp.int32, (owners, HDIM), 1)
+    pairs = dot(counts_ref[...].astype(F32).astype(BF), jnp.where(part_of == lanes, 1.0, 0.0).astype(BF))
+    plane = lax.broadcasted_iota(jnp.int32, (NZ, owners), 1) // ND
+    loads = dot(jnp.where(plane == lax.broadcasted_iota(jnp.int32, (NZ, owners), 0), 1.0, 0.0).astype(BF),
+                pairs.astype(BF))
+    fits = (jnp.max(loads) <= FAST[0]) & (jnp.max(pairs) <= FAST[1])
+    fits_ref[0] = fits.astype(jnp.int32)
+    pair = jnp.where(fits, FAST[1], SLOW[1])
+
+    ids = lax.broadcasted_iota(jnp.int32, (1, tok), 1)
+    slot = ids
+    start = jnp.int32(0)
+    filled = [jnp.int32(0)] * ND
+    for f in range(owners):
+        n = rc_ref[z * ND + d, f]
+        to = f % ND
+        slot = jnp.where(ids >= start, ids + (to * pair + filled[to] - start), slot)
+        filled[to] = filled[to] + n
+        start = start + n
+    slot_ref[...] = slot
+
+    start = jnp.int32(0)
+    for c in range(NZ):
+        for e in range(ND):
+            tops[e, c] = start
+            start = start + rc_ref[z * ND + e, c * ND + d]
+    ids = lax.broadcasted_iota(jnp.int32, idx_ref.shape, 1)
+    idx = ids
+    for e in range(ND):
+        start = e * pair
+        for c in range(NZ):
+            idx = jnp.where(ids >= start, ids + (tops[e, c] - start), idx)
+            start = start + rc_ref[z * ND + e, c * ND + d]
+        idx = jnp.where(ids >= start, -1, idx)
+    idx_ref[...] = idx
+
+    before = [jnp.int32(0)] * NZ
+    for c0 in range(NZ):
+        start = jnp.int32(0)
+        for c in range(NZ):
+            n = rc_ref[c0 * ND, c * ND + d]
+            for e in range(1, ND):
+                n = n + rc_ref[c0 * ND + e, c * ND + d]
+            tab_ref[c0, NZ + c] = c * tok + before[c] - start
+            start = start + n
+            before[c] = before[c] + n
+            tab_ref[c0, c] = start
+
+    def placed(ids, plane):
+        pos = ids + tab_ref[plane, NZ]
+        for c in range(1, NZ):
+            pos = jnp.where(ids >= tab_ref[plane, c - 1], ids + tab_ref[plane, NZ + c], pos)
+        return jnp.where(ids >= tab_ref[plane, NZ - 1], FAR, pos)
+
+    first = lax.broadcasted_iota(jnp.int32, (1, HDIM), 1) * KS
+    k_min = k_max = None
+    for c0 in range(NZ):
+        low, high = placed(first, c0), placed(first + (KS - 1), c0)
+        k_min = low if c0 == 0 else jnp.minimum(k_min, low)
+        k_max = high if c0 == 0 else jnp.maximum(k_max, high)
+    for b in range(qpos_ref.shape[0]):
+        pos = placed(lax.broadcasted_iota(jnp.int32, (1, QB), 1) + b * QB, z)
+        lo = jnp.zeros_like(pos)
+        bound = jnp.int32(0)
+        for m in range(doc_ref.shape[1]):
+            bound = bound + doc_ref[0, m]
+            lo = jnp.where(pos >= bound, bound, lo)
+        hi = jnp.where(pos < FAR, pos, -1)
+        qpos_ref[b, 0:1, :] = hi
+        qpos_ref[b, 1:2, :] = lo
+        q_max = jnp.max(hi.astype(F32)).astype(jnp.int32)
+        q_min = jnp.min(jnp.where(pos < FAR, lo, FAR).astype(F32)).astype(jnp.int32)
+        span_ref[0, b] = jnp.sum(jnp.where(k_max < q_min, 1.0, 0.0)).astype(jnp.int32)
+        span_ref[1, b] = jnp.sum(jnp.where(k_min <= q_max, 1.0, 0.0)).astype(jnp.int32)
+
+
+def tables(route_counts, doc_lengths, tok):
+    blocks = -(-SLOW[0] // QB)
+    i32 = jnp.int32
+    return pl.pallas_call(
+        functools.partial(tables_kernel, tok),
+        out_shape=(
+            jax.ShapeDtypeStruct((1, tok), i32), jax.ShapeDtypeStruct((1, ND * SLOW[1]), i32),
+            jax.ShapeDtypeStruct((blocks, 2, QB), i32), jax.ShapeDtypeStruct((NZ, 2 * NZ), i32),
+            jax.ShapeDtypeStruct((2, blocks), i32), jax.ShapeDtypeStruct((1,), i32),
+        ),
+        in_specs=[SMEM_SPEC, VMEM_SPEC, SMEM_SPEC],
+        out_specs=(VMEM_SPEC,) * 3 + (SMEM_SPEC,) * 3,
+        scratch_shapes=[pltpu.SMEM((ND, NZ), i32)],
+        name="routing_tables",
+    )(route_counts, route_counts, doc_lengths)
 
 
 def greet():
@@ -173,7 +221,7 @@
     own[0].wait()
     for c in kv_copies:
         c.wait_recv()
-    mine[...] = dot(one_hot_rows(cap, idx_ref[...]), rkv[...].reshape(slots, 2 * kvw)).astype(BF)
+    mine[...] = dot(one_hot_rows(cap, idx_ref[:, :slots]), rkv[...].reshape(slots, 2 * kvw)).astype(BF)
     sent = []
 
     def hop(step, piece):
@@ -252,7 +300,7 @@
         c = pltpu.make_async_copy(src, dst, ins.at[n])
         c.start()
         loads.append(c)
-    pick = one_hot_rows(capq, row_ref[...])
+    pick = one_hot_rows(capq, row_ref[:, :rq_ref.shape[0]])
     ids = lax.broadcasted_iota(jnp.int32, (cap, HDIM), 0)
     for z in range(NZ):
         p = ids + tab_ref[z, NZ]
@@ -311,17 +359,18 @@
 
     lax.fori_loop(0, nq, q_block, 0)
     dkv_ref[...] = dkv[...].astype(BF)
+    back = pick.T
     for h in range(0, heads, 2):
         cols = []
         for e in range(2):
             g, r = divmod(h + e, group)
             cols.append(jnp.concatenate([dq[g, i, r * QB:(r + 1) * QB, :] for i in range(nq)], axis=0).astype(BF))
-        dq_ref[:, h * HDIM:(h + 2) * HDIM] = dot_rows(pick, jnp.concatenate(cols, axis=1)).astype(BF)
+        dq_ref[:, h * HDIM:(h + 2) * HDIM] = dot(back, jnp.concatenate(cols, axis=1)).astype(BF)
 
 
 def attend(span, tab, kv_all, rq, rg, idx_row, qpos, group, kvh):
     cap, kvw = kv_all.shape[1:]
-    nq = qpos.shape[0]
+    nq = -(-cap // QB)
     slots, width = rq.shape
     return pl.pallas_call(
         functools.partial(attend_kernel, group, kvh),
@@ -391,7 +440,7 @@
         if s == last:
             c.wait_recv()
     total = (dkv_ref[z].astype(F32) + fin[last].astype(F32) + bin_[last].astype(F32)).astype(BF)
-    slots[...] = dot_rows(one_hot_rows(cap, idx_ref[...]), total).astype(BF).reshape(slots.shape)
+    slots[...] = dot_rows(one_hot_rows(cap, idx_ref[:, :ND * slots.shape[1]]), total).astype(BF).reshape(slots.shape)
     kv_copies = exchange(slots, rdkv_ref, ks, kr)
     for c in kv_copies:
         c.start()
@@ -430,14 +479,23 @@
     )(dkv, dq, idx_row)
 
 
-def unpack_kernel(dq_ref, dkv_ref, slot_ref, gq_ref, gk_ref, gv_ref):
+def unpack_kernel(dq_hbm, dkv_hbm, slot_ref, gq_ref, gk_ref, gv_ref, dq_ref, dkv_ref, ins):
     slots, width = dq_ref.shape
     kvw = gk_ref.shape[1]
-    pick = one_hot_rows(slots, slot_ref[...])
-    for at in range(0, width, 2 * HDIM):
-        gq_ref[:, at:at + 2 * HDIM] = dot_rows(pick, dq_ref[:, at:at + 2 * HDIM]).astype(BF)
-    gk_ref[...] = dot_rows(pick, dkv_ref[:, :kvw]).astype(BF)
-    gv_ref[...] = dot_rows(pick, dkv_ref[:, kvw:]).astype(BF)
+    blocks = range(0, width, 2 * HDIM)
+    loads = [pltpu.make_async_copy(dkv_hbm, dkv_ref, ins.at[len(blocks)])]
+    for n, at in enumerate(blocks):
+        at = pl.ds(at, 2 * HDIM)
+        loads.append(pltpu.make_async_copy(dq_hbm.at[:, at], dq_ref.at[:, at], ins.at[n]))
+    for c in loads:
+        c.start()
+    pick = one_hot_rows(slots, slot_ref[...]).T
+    loads[0].wait()
+    gk_ref[...] = dot(pick, dkv_ref[:, :kvw]).astype(BF)
+    gv_ref[...] = dot(pick, dkv_ref[:, kvw:]).astype(BF)
+    for n, at in enumerate(blocks):
+        loads[n + 1].wait()
+        gq_ref[:, at:at + 2 * HDIM] = dot(pick, dq_ref[:, at:at + 2 * HDIM]).astype(BF)
 
 
 def unpack(rdq, rdkv, slot_row):
@@ -452,9 +510,13 @@
             jax.ShapeDtypeStruct((tok, kvw), BF),
             jax.ShapeDtypeStruct((tok, kvw), BF),
         ),
-        in_specs=[VMEM_SPEC] * 3,
+        in_specs=[ANY_SPEC, ANY_SPEC, VMEM_SPEC],
         out_specs=(VMEM_SPEC,) * 3,
-        compiler_params=pltpu.CompilerParams(vmem_limit_bytes=32 << 20),
+        scratch_shapes=[
+            pltpu.VMEM((slots, width), BF), pltpu.VMEM((slots, 2 * kvw), BF),
+            pltpu.SemaphoreType.DMA((width // (2 * HDIM) + 1,)),
+        ],
+        compiler_params=pltpu.CompilerParams(vmem_limit_bytes=56 << 20),
         name="unpack_rows",
     )(rdq.reshape(slots, width), rdkv.reshape(slots, 2 * kvw), slot_row)
 
@@ -463,37 +525,17 @@
     tok = query.shape[0]
     kvh = keys.shape[1] // HDIM
     group = query.shape[1] // keys.shape[1]
-    loads = jnp.sum(route_counts.reshape(NZ, ND, NZ, ND), axis=2)
-    fits = (jnp.max(jnp.sum(loads, axis=1)) <= FAST[0]) & (jnp.max(loads) <= FAST[1])
+    slot, idx, qpos, tab, span, fits = tables(route_counts, doc_lengths, tok)
 
     def run(size, cid, *rows):
         cap, pair = size
-        capq = -(-cap // QB) * QB
-        q = plane_counts(route_counts)
-        slot = source_slots(route_counts, tok, pair).reshape(1, -1)
-        idx = compact_index(q, pair).reshape(1, -1)
-        pos, tab = positions(q, cap, tok)
-        mine = lax.dynamic_index_in_dim(pos, lax.axis_index("ctx"), 0, keepdims=False)
-        mine = jnp.pad(mine, (0, capq - cap), constant_values=FAR)
-        bounds = ends_of(doc_lengths[0], 0)
-        lo = jnp.max(jnp.where(bounds[None, :] <= mine[:, None], bounds[None, :], 0), axis=1)
-        hi = jnp.where(mine < FAR, mine, -1)
-        qpos = jnp.stack([hi.reshape(-1, QB), lo.reshape(-1, QB)], axis=1)
-        k_tiles = pos.reshape(NZ, -1, KS)
-        k_min = jnp.min(k_tiles, axis=(0, 2))
-        k_max = jnp.max(k_tiles, axis=(0, 2))
-        q_max = jnp.max(qpos[:, 0, :], axis=1)
-        q_min = jnp.min(jnp.where(qpos[:, 0, :] >= 0, qpos[:, 1, :], FAR), axis=1)
-        span = jnp.stack([
-            jnp.sum((k_max[None, :] < q_min[:, None]).astype(jnp.int32), axis=1),
-            jnp.sum((k_min[None, :] <= q_max[:, None]).astype(jnp.int32), axis=1)])
+        slots = ND * pair
         kv_all, rq, rg = dispatch(*rows, slot, idx, cap, pair, cid)
-        slots = ND * pair
         dkv, dq = attend(span, tab, kv_all, rq.reshape(slots, -1), rg.reshape(slots, -1), idx, qpos, group, kvh)
         rdq, rdkv = send_back(dkv, dq.reshape(ND, pair, -1), idx, cid + 1)
         return unpack(rdq, rdkv, slot)
 
-    return lax.cond(fits, functools.partial(run, FAST, 0), functools.partial(run, SLOW, 2),
+    return lax.cond(fits[0] > 0, functools.partial(run, FAST, 0), functools.partial(run, SLOW, 2),
                     query, keys, values, output, grad_out, log_norm)
 
 

time: 174 us -> 164 us (0.943)
  other arithmetic: 8.37 us -> 0 us
  local copies, waits for them, and re-layouts: 8.17 us -> 0 us
  Pallas kernels: 154 us -> 160 us
    pallas_call x1, Pallas kernels: 54 us -> 50.1 us  [send_back(): pl.pallas_call(return_kernel, out_shape=(jax.ShapeDtypeStruct((ND, pair,...]
    pallas_call x0 -> x1, Pallas kernels: none -> 3.91 us  [tables(): pl.pallas_call(functools.partial(tables_kernel, tok), out_shape=(jax.Shap...]
    pallas_call x1, Pallas kernels: 1.95 us -> 4.87 us  [unpack(): pl.pallas_call(unpack_kernel, out_shape=(jax.ShapeDtypeStruct((tok, width...]
    reduce_sum x11 -> x0, other arithmetic: 2.55 us -> none  [the longest x4 1.63 us: ends_of(): out = jnp.sum(jnp.where(tri, x[..., None, :], 0), axis=-1)]
    cond x6 -> x0, local copies, waits for them, and re-layouts: 2.51 us -> none
    pallas_call x1, Pallas kernels: 33.3 us -> 35.4 us  [attend(): pl.pallas_call(functools.partial(attend_kernel, group, kvh), out_shape=(j...]
where the time goes in v3:
time: 164 us; the launch traced here: 162 us
  Pallas kernels  160 us (98%)
    pallas_call x1, Pallas kernels, dispatch(): pl.pallas_call(dispatch_kernel, out_shape=(jax.ShapeDtypeStruct((NZ, cap,...  65.2 us
    pallas_call x1, Pallas kernels, send_back(): pl.pallas_call(return_kernel, out_shape=(jax.ShapeDtypeStruct((ND, pair,...  50.1 us
    pallas_call x1, Pallas kernels, attend(): pl.pallas_call(functools.partial(attend_kernel, group, kvh), out_shape=(j...  35.4 us
    pallas_call x1, Pallas kernels, unpack(): pl.pallas_call(unpack_kernel, out_shape=(jax.ShapeDtypeStruct((tok, width...  4.87 us
    pallas_call x1, Pallas kernels, tables(): pl.pallas_call(functools.partial(tables_kernel, tok), out_shape=(jax.Shap...  3.91 us

profile of v3, /device:TPU:4, one launch (start us, length us, event | category | flops | bytes accessed | tf_op | source)
XLA Modules:
  0.0 161.6 jit_solution(12440325419640637250)
XLA Ops:
  0.6 3.9 %routing_tables.1 = (s32[1,352]{1,0:T(1,128)S(1)}, s32[1,704]{1,0:T(1,128)S(1)}, s32[6,2,128]{2,1,0:T(2,128)S(1)}, s32[8,16]{1,0:T(8,128)S(1)}, s32[2,6]{1,0:T(2,128)S(1)}, /*index=5*/s32[1]{0:T(128)}) custom-call(s32[64,64]{1,0:T(8,128)} %counts_ref.1, s32[64,64]{1,0:T(8,128)} %counts_ref.1, s32[1,4]{1,0:T(1,128)} %doc_ref.1), custom_call_target="tpu_custom_call" | custom-call | tf_op jit(solution)/shard_map/routing_tables/pallas_call | solution.py:124
  5.2 156.2 %conditional.1 = ((bf16[352,1280]{1,0:T(8,128)(2,1)}, bf16[352,256]{1,0:T(8,128)(2,1)}, bf16[352,256]{1,0:T(8,128)(2,1)})) conditional(s32[]{:T(128)} %bitcast.12, (bf16[352,10]{0,1:T(8,128)(2,1)}, bf16[352,1280]{1,0:T(8,128)(2,1)}, bf16[352,256]{1,0:T(8,128)(2,1)}, bf16[352,256]{1,0:T(8,128)(2,1)}, bf16[352,1280]{1,0:T(8,128)(2,1)}, ...), branch_computations={%region_0.0_spmd, %region_1.0_spmd} | conditional | bytes 8 | solution.py:538
  5.4 65.2 %dispatch_rows.3 = (bf16[8,448,512]{2,1,0:T(8,128)(2,1)}, bf16[8,80,1280]{2,1,0:T(8,128)(2,1)}, bf16[8,80,1408]{2,1,0:T(8,128)(2,1)}) custom-call(bf16[352,1280]{1,0:T(8,128)(2,1)} %get-tuple-element.64.q_ref, bf16[352,256]{1,0:T(8,128)(2,1)} %get-tuple-element.65.k_ref, bf16[352,256]{1,0:T(8,128)(2,1)} %get-tuple-element.66.v_ref, ...), custom_call_target="tpu_custom_call" | custom-call | tf_op jit(solution)/shard_map/cond/branch_1_fun/dispatch_rows/pallas_call | solution.py:265
  70.7 35.4 %attention_grads.3 = (bf16[8,448,512]{2,1,0:T(8,128)(2,1)}, bf16[640,1280]{1,0:T(8,128)(2,1)}) custom-call(s32[2,6]{1,0:T(2,128)S(1)} %get-tuple-element.62.span_ref, s32[8,16]{1,0:T(8,128)S(1)} %get-tuple-element.63.tab_ref, bf16[8,448,512]{2,1,0:T(8,128)(2,1)} %get-tuple-element.72.all_hbm, bf16[640,1280]{1,0:T(8,128)(2,1)} %bitcast.20, ...), custom_call_target="tpu_custom_call" | custom-call | tf_op jit(solution)/shard_map/cond/branch_1_fun/attention_grads/pallas_call | solution.py:375
  106.1 50.1 %return_rows.3 = (bf16[8,80,1280]{2,1,0:T(8,128)(2,1)}, bf16[8,80,512]{2,1,0:T(8,128)(2,1)}) custom-call(bf16[8,448,512]{2,1,0:T(8,128)(2,1)} %get-tuple-element.76.dkv_hbm, bf16[8,80,1280]{2,1,0:T(8,128)(2,1)} %bitcast.18, s32[1,704]{1,0:T(1,128)S(1)} %get-tuple-element.71.idx_ref.row_ref), custom_call_target="tpu_custom_call" | custom-call | tf_op jit(solution)/shard_map/cond/branch_1_fun/return_rows/pallas_call | solution.py:463
  156.2 4.9 %unpack_rows.3 = (bf16[352,1280]{1,0:T(8,128)(2,1)}, bf16[352,256]{1,0:T(8,128)(2,1)}, bf16[352,256]{1,0:T(8,128)(2,1)}) custom-call(bf16[640,1280]{1,0:T(8,128)(2,1)} %bitcast.19, bf16[640,512]{1,0:T(8,128)(2,1)} %bitcast.22, s32[1,352]{1,0:T(1,128)S(1)} %get-tuple-element.70.slot_ref), custom_call_target="tpu_custom_call" | custom-call | tf_op jit(solution)/shard_map/cond/branch_1_fun/unpack_rows/pallas_call | solution.py:506

commit v4 on v3

--- a/solution.py
+++ b/solution.py
@@ -285,8 +285,8 @@
     )(query, keys, values, output, grad_out, log_norm.T, slot_row, idx_row)
 
 
-def attend_kernel(group, kvh, span_ref, tab_ref, all_hbm, rq_hbm, rg_hbm, row_ref, qpos_ref, dkv_ref, dq_ref,
-                  all_ref, rq_ref, rg_ref, qs, gs, lse, dlt, dq, dkv, kpos, ins):
+def attend_kernel(group, kvh, span_ref, tab_ref, all_hbm, rq_hbm, rg_hbm, row_ref, qpos_ref, dkv_hbm, dq_hbm,
+                  all_ref, rq_ref, rg_ref, qs, gs, lse, dlt, dq, dkv, kpos, dkv_ref, dq_ref, ins):
     nq = qs.shape[1]
     capq = nq * QB
     heads = group * kvh
@@ -359,6 +359,8 @@
 
     lax.fori_loop(0, nq, q_block, 0)
     dkv_ref[...] = dkv[...].astype(BF)
+    outs = [pltpu.make_async_copy(dkv_ref, dkv_hbm, ins.at[3])]
+    outs[0].start()
     back = pick.T
     for h in range(0, heads, 2):
         cols = []
@@ -366,6 +368,10 @@
             g, r = divmod(h + e, group)
             cols.append(jnp.concatenate([dq[g, i, r * QB:(r + 1) * QB, :] for i in range(nq)], axis=0).astype(BF))
         dq_ref[:, h * HDIM:(h + 2) * HDIM] = dot(back, jnp.concatenate(cols, axis=1)).astype(BF)
+    outs.append(pltpu.make_async_copy(dq_ref, dq_hbm, ins.at[4]))
+    outs[1].start()
+    for c in outs:
+        c.wait()
 
 
 def attend(span, tab, kv_all, rq, rg, idx_row, qpos, group, kvh):
@@ -379,22 +385,23 @@
             jax.ShapeDtypeStruct((slots, width), BF),
         ),
         in_specs=[SMEM_SPEC] * 2 + [ANY_SPEC] * 3 + [VMEM_SPEC] * 2,
-        out_specs=(VMEM_SPEC, VMEM_SPEC),
+        out_specs=(ANY_SPEC, ANY_SPEC),
         scratch_shapes=[
             pltpu.VMEM((NZ, cap, kvw), BF), pltpu.VMEM(rq.shape, BF), pltpu.VMEM(rg.shape, BF),
             pltpu.VMEM((kvh, nq, group * QB, HDIM), BF), pltpu.VMEM((kvh, nq, group * QB, HDIM), BF),
             pltpu.VMEM((kvh, nq, 8, group * QB), F32), pltpu.VMEM((kvh, nq, 8, group * QB), F32),
             pltpu.VMEM((kvh, nq, group * QB, HDIM), F32), pltpu.VMEM((NZ, cap, kvw), F32),
             pltpu.VMEM((NZ, cap, HDIM), jnp.int32),
-            pltpu.SemaphoreType.DMA((3,)),
+            pltpu.VMEM((NZ, cap, kvw), BF), pltpu.VMEM((slots, width), BF),
+            pltpu.SemaphoreType.DMA((5,)),
         ],
         compiler_params=pltpu.CompilerParams(vmem_limit_bytes=60 << 20),
         name="attention_grads",
     )(span, tab, kv_all, rq, rg, idx_row, qpos)
 
 
-def return_kernel(dkv_hbm, dq_ref, idx_ref, rdq_ref, rdkv_ref, dkv_ref, fin, bin_, fout, bout, slots,
-                  qs, qr, ks, kr, ls, fs, fr, bs, br):
+def return_kernel(dkv_hbm, dq_ref, idx_ref, slot_ref, gq_ref, gk_ref, gv_ref,
+                  dkv_ref, fin, bin_, fout, bout, slots, rdq_ref, rdkv_ref, gq, gk, gv, qs, qr, ks, kr, ls, fs, fr, bs, br):
     z = lax.axis_index("ctx")
     d = lax.axis_index("dp")
     cap, kvw = dkv_ref.shape[1:]
@@ -436,6 +443,15 @@
     for step in range(1, NZ // 2):
         hop(step, 0)
         hop(step, 1)
+    own.wait()
+    for c in dq_copies:
+        c.wait()
+    count, width = slots.shape[0] * slots.shape[1], gq.shape[1]
+    pick = one_hot_rows(count, slot_ref[...]).T
+    rows = rdq_ref[...].reshape(count, width)
+    gq[...] = dot(pick, rows).astype(BF)
+    outs = [pltpu.make_async_copy(gq, gq_ref, ls.at[3])]
+    outs[0].start()
     for s, p, b, c in sent:
         if s == last:
             c.wait_recv()
@@ -448,77 +464,44 @@
     own_kv.start()
     for s, p, b, c in sent:
         c.wait_send()
-    own.wait()
     own_kv.wait()
-    for c in dq_copies:
-        c.wait()
     for c in kv_copies:
         c.wait()
-
-
-def send_back(dkv, dq, idx_row, cid):
+    rows = rdkv_ref[...].reshape(count, kvw)
+    gk[...] = dot(pick, rows[:, :kvw // 2]).astype(BF)
+    gv[...] = dot(pick, rows[:, kvw // 2:]).astype(BF)
+    outs.append(pltpu.make_async_copy(gk, gk_ref, ls.at[4]))
+    outs.append(pltpu.make_async_copy(gv, gv_ref, ls.at[5]))
+    for c in outs[1:]:
+        c.start()
+    for c in outs:
+        c.wait()
+
+
+def send_back(dkv, dq, idx_row, slot_row, cid):
     cap, kvw = dkv.shape[1:]
     pair, width = dq.shape[1:]
+    tok = slot_row.shape[1]
     dma = pltpu.SemaphoreType.DMA
     return pl.pallas_call(
         return_kernel,
         out_shape=(
-            jax.ShapeDtypeStruct((ND, pair, width), BF),
-            jax.ShapeDtypeStruct((ND, pair, kvw), BF),
+            jax.ShapeDtypeStruct((tok, width), BF),
+            jax.ShapeDtypeStruct((tok, kvw // 2), BF),
+            jax.ShapeDtypeStruct((tok, kvw // 2), BF),
         ),
-        in_specs=[ANY_SPEC, ANY_SPEC, VMEM_SPEC],
-        out_specs=(ANY_SPEC, ANY_SPEC),
+        in_specs=[ANY_SPEC, ANY_SPEC, VMEM_SPEC, VMEM_SPEC],
+        out_specs=(ANY_SPEC,) * 3,
         scratch_shapes=[pltpu.VMEM((NZ, cap, kvw), BF)] + [pltpu.VMEM((NZ // 2, cap, kvw), BF)] * 4 + [
-            pltpu.VMEM((ND, pair, kvw), BF),
-            dma((ND,)), dma((ND,)), dma((ND,)), dma((ND,)), dma((3,)),
+            pltpu.VMEM((ND, pair, kvw), BF), pltpu.VMEM((ND, pair, width), BF), pltpu.VMEM((ND, pair, kvw), BF),
+            pltpu.VMEM((tok, width), BF), pltpu.VMEM((tok, kvw // 2), BF), pltpu.VMEM((tok, kvw // 2), BF),
+            dma((ND,)), dma((ND,)), dma((ND,)), dma((ND,)), dma((6,)),
             dma((4, 2)), dma((4, 2)), dma((4, 2)), dma((4, 2)),
         ],
         compiler_params=pltpu.CompilerParams(
             collective_id=cid, has_side_effects=True, vmem_limit_bytes=56 << 20),
         name="return_rows",
-    )(dkv, dq, idx_row)
-
-
-def unpack_kernel(dq_hbm, dkv_hbm, slot_ref, gq_ref, gk_ref, gv_ref, dq_ref, dkv_ref, ins):
-    slots, width = dq_ref.shape
-    kvw = gk_ref.shape[1]
-    blocks = range(0, width, 2 * HDIM)
-    loads = [pltpu.make_async_copy(dkv_hbm, dkv_ref, ins.at[len(blocks)])]
-    for n, at in enumerate(blocks):
-        at = pl.ds(at, 2 * HDIM)
-        loads.append(pltpu.make_async_copy(dq_hbm.at[:, at], dq_ref.at[:, at], ins.at[n]))
-    for c in loads:
-        c.start()
-    pick = one_hot_rows(slots, slot_ref[...]).T
-    loads[0].wait()
-    gk_ref[...] = dot(pick, dkv_ref[:, :kvw]).astype(BF)
-    gv_ref[...] = dot(pick, dkv_ref[:, kvw:]).astype(BF)
-    for n, at in enumerate(blocks):
-        loads[n + 1].wait()
-        gq_ref[:, at:at + 2 * HDIM] = dot(pick, dq_ref[:, at:at + 2 * HDIM]).astype(BF)
-
-
-def unpack(rdq, rdkv, slot_row):
-    tok = slot_row.shape[1]
-    slots = rdq.shape[0] * rdq.shape[1]
-    width = rdq.shape[2]
-    kvw = rdkv.shape[2] // 2
-    return pl.pallas_call(
-        unpack_kernel,
-        out_shape=(
-            jax.ShapeDtypeStruct((tok, width), BF),
-            jax.ShapeDtypeStruct((tok, kvw), BF),
-            jax.ShapeDtypeStruct((tok, kvw), BF),
-        ),
-        in_specs=[ANY_SPEC, ANY_SPEC, VMEM_SPEC],
-        out_specs=(VMEM_SPEC,) * 3,
-        scratch_shapes=[
-            pltpu.VMEM((slots, width), BF), pltpu.VMEM((slots, 2 * kvw), BF),
-            pltpu.SemaphoreType.DMA((width // (2 * HDIM) + 1,)),
-        ],
-        compiler_params=pltpu.CompilerParams(vmem_limit_bytes=56 << 20),
-        name="unpack_rows",
-    )(rdq.reshape(slots, width), rdkv.reshape(slots, 2 * kvw), slot_row)
+    )(dkv, dq, idx_row, slot_row)
 
 
 def body(query, keys, values, output, grad_out, log_norm, route_counts, doc_lengths):
@@ -532,8 +515,7 @@
         slots = ND * pair
         kv_all, rq, rg = dispatch(*rows, slot, idx, cap, pair, cid)
         dkv, dq = attend(span, tab, kv_all, rq.reshape(slots, -1), rg.reshape(slots, -1), idx, qpos, group, kvh)
-        rdq, rdkv = send_back(dkv, dq.reshape(ND, pair, -1), idx, cid + 1)
-        return unpack(rdq, rdkv, slot)
+        return send_back(dkv, dq.reshape(ND, pair, -1), idx, slot, cid + 1)
 
     return lax.cond(fits[0] > 0, functools.partial(run, FAST, 0), functools.partial(run, SLOW, 2),
                     query, keys, values, output, grad_out, log_norm)

time: 164 us -> 163 us (level)
  local copies, waits for them, and re-layouts: 0 us -> 2.26 us
  Pallas kernels: 160 us -> 158 us
    pallas_call x2 -> x1, Pallas kernels: 54.9 us -> 47.3 us  [send_back(): pl.pallas_call(return_kernel, out_shape=(jax.ShapeDtypeStruct((tok, width...]
    pallas_call x1, Pallas kernels: 35.4 us -> 41.4 us  [attend(): pl.pallas_call(functools.partial(attend_kernel, group, kvh), out_shape=(j...]
    unnamed x0 -> x3, local copies, waits for them, and re-layouts: none -> 2.26 us
where the time goes in v4:
time: 163 us; the launch traced here: 162 us
  Pallas kernels  158 us (97%)
  local copies, waits for them, and re-layouts  2.26 us (1%)
    pallas_call x1, Pallas kernels, dispatch(): pl.pallas_call(dispatch_kernel, out_shape=(jax.ShapeDtypeStruct((NZ, cap,...  65.2 us
    pallas_call x1, Pallas kernels, send_back(): pl.pallas_call(return_kernel, out_shape=(jax.ShapeDtypeStruct((tok, width...  47.3 us
    pallas_call x1, Pallas kernels, attend(): pl.pallas_call(functools.partial(attend_kernel, group, kvh), out_shape=(j...  41.4 us
    pallas_call x1, Pallas kernels, tables(): pl.pallas_call(functools.partial(tables_kernel, tok), out_shape=(jax.Shap...  3.91 us

profile of v4, /device:TPU:4, one launch (start us, length us, event | category | flops | bytes accessed | tf_op | source)
XLA Modules:
  0.0 161.7 jit_solution(3118365940936152490)
XLA Ops:
  0.6 3.9 %routing_tables.1 = (s32[1,352]{1,0:T(1,128)S(1)}, s32[1,704]{1,0:T(1,128)S(1)}, s32[6,2,128]{2,1,0:T(2,128)S(1)}, s32[8,16]{1,0:T(8,128)S(1)}, s32[2,6]{1,0:T(2,128)S(1)}, /*index=5*/s32[1]{0:T(128)}) custom-call(s32[64,64]{1,0:T(8,128)} %counts_ref.1, s32[64,64]{1,0:T(8,128)} %counts_ref.1, s32[1,4]{1,0:T(1,128)} %doc_ref.1), custom_call_target="tpu_custom_call" | custom-call | tf_op jit(solution)/shard_map/routing_tables/pallas_call | solution.py:124
  5.2 154.2 %conditional.1 = ((bf16[352,1280]{1,0:T(8,128)(2,1)S(1)}, bf16[352,256]{1,0:T(8,128)(2,1)S(1)}, bf16[352,256]{1,0:T(8,128)(2,1)S(1)})) conditional(s32[]{:T(128)} %bitcast.8, (bf16[352,10]{0,1:T(8,128)(2,1)}, bf16[352,1280]{1,0:T(8,128)(2,1)}, bf16[352,256]{1,0:T(8,128)(2,1)}, bf16[352,256]{1,0:T(8,128)(2,1)}, bf16[352,1280]{1,0:T(8,128)(2,1)}, ...), branch_computations={%region_0.0_spmd, %region_1.0_spmd} | conditional | bytes 8 | solution.py:520
  5.4 65.2 %dispatch_rows.3 = (bf16[8,448,512]{2,1,0:T(8,128)(2,1)}, bf16[8,80,1280]{2,1,0:T(8,128)(2,1)}, bf16[8,80,1408]{2,1,0:T(8,128)(2,1)}) custom-call(bf16[352,1280]{1,0:T(8,128)(2,1)} %get-tuple-element.62.q_ref, bf16[352,256]{1,0:T(8,128)(2,1)} %get-tuple-element.63.k_ref, bf16[352,256]{1,0:T(8,128)(2,1)} %get-tuple-element.64.v_ref, ...), custom_call_target="tpu_custom_call" | custom-call | tf_op jit(solution)/shard_map/cond/branch_1_fun/dispatch_rows/pallas_call | solution.py:265
  70.7 41.4 %attention_grads.3 = (bf16[8,448,512]{2,1,0:T(8,128)(2,1)}, bf16[640,1280]{1,0:T(8,128)(2,1)}) custom-call(s32[2,6]{1,0:T(2,128)S(1)} %get-tuple-element.60.span_ref, s32[8,16]{1,0:T(8,128)S(1)} %get-tuple-element.61.tab_ref, bf16[8,448,512]{2,1,0:T(8,128)(2,1)} %get-tuple-element.70.all_hbm, bf16[640,1280]{1,0:T(8,128)(2,1)} %bitcast.14, ...), custom_call_target="tpu_custom_call" | custom-call | tf_op jit(solution)/shard_map/cond/branch_1_fun/attention_grads/pallas_call | solution.py:381
  112.1 47.3 %return_rows.3 = (bf16[352,1280]{1,0:T(8,128)(2,1)S(1)}, bf16[352,256]{1,0:T(8,128)(2,1)S(1)}, bf16[352,256]{1,0:T(8,128)(2,1)S(1)}) custom-call(bf16[8,448,512]{2,1,0:T(8,128)(2,1)} %get-tuple-element.74.dkv_hbm, bf16[8,80,1280]{2,1,0:T(8,128)(2,1)} %bitcast.13, s32[1,704]{1,0:T(1,128)S(1)} %get-tuple-element.69.idx_ref.row_ref, ...), custom_call_target="tpu_custom_call" | custom-call | tf_op jit(solution)/shard_map/cond/branch_1_fun/return_rows/pallas_call | solution.py:486
  159.4 0.9 copy.26
  160.3 0.7 copy.27
  161.0 0.7 copy.28

commit v5 on v4

--- a/solution.py
+++ b/solution.py
@@ -165,32 +165,33 @@
 
 
 def dispatch_kernel(q_ref, k_ref, v_ref, o_ref, g_ref, l_ref, slot_ref, idx_ref, all_ref, rq_ref, rg_ref,
-                    qv, kvv, ov, gv, stat, skv, sq, sg, rkv, mine,
-                    ins, ks, kr, qs, qr, gs, gr, ls, fs, fr, bs, br):
+                    qv, kv, vv, ov, gv, stat, sk, sv, sq, sg, rk, rv, mine,
+                    ins, ks, kr, vs, vr, qs, qr, gs, gr, ls, fs, fr, bs, br):
     z = lax.axis_index("ctx")
     d = lax.axis_index("dp")
     width = qv.shape[1]
     heads = width // HDIM
     kvw = k_ref.shape[1]
-    slots, pair = skv.shape[0] * skv.shape[1], skv.shape[1]
+    slots, pair = sk.shape[0] * sk.shape[1], sk.shape[1]
     cap = mine.shape[0]
-    part = cap // 2
     loads = []
-    for n, (src, dst) in enumerate(((k_ref, kvv.at[:, :kvw]), (v_ref, kvv.at[:, kvw:]),
-                                    (q_ref, qv), (g_ref, gv), (o_ref, ov))):
+    for n, (src, dst) in enumerate(((k_ref, kv), (v_ref, vv), (q_ref, qv), (g_ref, gv), (o_ref, ov))):
         c = pltpu.make_async_copy(src, dst, ins.at[n])
         c.start()
         loads.append(c)
     greet()
     pick = one_hot_rows(slots, slot_ref[...])
-    loads[0].wait()
-    loads[1].wait()
-    skv[...] = dot(pick, kvv[...]).astype(BF).reshape(skv.shape)
-    kv_copies = exchange(skv, rkv, ks, kr)
-    for c in kv_copies:
-        c.start()
-    own = [pltpu.make_async_copy(skv.at[d], rkv.at[d], ls.at[0])]
-    own[0].start()
+    kv_copies = []
+    own = []
+    for n, (src, out, into, send, recv) in enumerate(((kv, sk, rk, ks, kr), (vv, sv, rv, vs, vr))):
+        loads[n].wait()
+        out[...] = dot(pick, src[...]).astype(BF).reshape(out.shape)
+        copies = exchange(out, into, send, recv)
+        for c in copies:
+            c.start()
+        kv_copies.append(copies)
+        own.append(pltpu.make_async_copy(out.at[d], into.at[d], ls.at[n]))
+        own[n].start()
     loads[2].wait()
     for at in range(0, width, 2 * HDIM):
         at = slice(at, at + 2 * HDIM)
@@ -198,8 +199,8 @@
     q_copies = exchange(sq, rq_ref, qs, qr)
     for c in q_copies:
         c.start()
-    own.append(pltpu.make_async_copy(sq.at[d], rq_ref.at[d], ls.at[1]))
-    own[1].start()
+    own.append(pltpu.make_async_copy(sq.at[d], rq_ref.at[d], ls.at[2]))
+    own[2].start()
     loads[3].wait()
     loads[4].wait()
     stat[...] = jnp.zeros_like(stat)
@@ -216,29 +217,30 @@
     g_copies = exchange(sg, rg_ref, gs, gr)
     for c in g_copies:
         c.start()
-    own.append(pltpu.make_async_copy(sg.at[d], rg_ref.at[d], ls.at[2]))
-    own[2].start()
-    own[0].wait()
-    for c in kv_copies:
-        c.wait_recv()
-    mine[...] = dot(one_hot_rows(cap, idx_ref[:, :slots]), rkv[...].reshape(slots, 2 * kvw)).astype(BF)
+    own.append(pltpu.make_async_copy(sg.at[d], rg_ref.at[d], ls.at[3]))
+    own[3].start()
     sent = []
 
     def hop(step, piece):
-        rows = pl.ds(piece * part, part)
+        cols = pl.ds(piece * kvw, kvw)
         for by, origin, send, recv, half in (
                 (1, lax.rem(z - step + NZ, NZ), fs, fr, 0), (NZ - 1, lax.rem(z + step, NZ), bs, br, 1)):
             if step == NZ // 2 - 1 and piece != half:
                 continue
-            src = mine.at[rows] if step == 0 else all_ref.at[origin, rows]
-            c = along(by, src, all_ref.at[origin, rows], send.at[step, piece], recv.at[step, piece])
+            src = mine.at[:, cols] if step == 0 else all_ref.at[origin, :, cols]
+            c = along(by, src, all_ref.at[origin, :, cols], send.at[step, piece], recv.at[step, piece])
             c.start()
             sent.append((step, piece, c))
 
-    for piece in range(2):
+    gather = one_hot_rows(cap, idx_ref[:, :slots])
+    for piece, into in enumerate((rk, rv)):
+        own[piece].wait()
+        for c in kv_copies[piece]:
+            c.wait_recv()
+        mine[:, piece * kvw:(piece + 1) * kvw] = dot(gather, into[...].reshape(slots, kvw)).astype(BF)
         hop(0, piece)
-    own.append(pltpu.make_async_copy(mine, all_ref.at[z], ls.at[3]))
-    own[3].start()
+    own.append(pltpu.make_async_copy(mine, all_ref.at[z], ls.at[4]))
+    own[4].start()
     for step in range(1, NZ // 2):
         for piece in range(2):
             for s, p, c in list(sent):
@@ -249,11 +251,11 @@
         if s == NZ // 2 - 1:
             c.wait_recv()
         c.wait_send()
-    for c in kv_copies:
+    for c in kv_copies[0] + kv_copies[1]:
         c.wait_send()
     for c in q_copies + g_copies:
         c.wait()
-    for c in own[1:]:
+    for c in own[2:]:
         c.wait()
 
 
@@ -272,11 +274,13 @@
         in_specs=[ANY_SPEC] * 5 + [VMEM_SPEC] * 3,
         out_specs=(ANY_SPEC,) * 3,
         scratch_shapes=[
-            pltpu.VMEM((tok, width), BF), pltpu.VMEM((tok, kvw), BF),
+            pltpu.VMEM((tok, width), BF), pltpu.VMEM((tok, kvw // 2), BF), pltpu.VMEM((tok, kvw // 2), BF),
             pltpu.VMEM((tok, width), BF), pltpu.VMEM((tok, width), BF), pltpu.VMEM((tok, HDIM), F32),
-            pltpu.VMEM((ND, pair, kvw), BF), pltpu.VMEM((ND, pair, width), BF), pltpu.VMEM((ND, pair, gw), BF),
-            pltpu.VMEM((ND, pair, kvw), BF), pltpu.VMEM((cap, kvw), BF),
-            dma((5,)), dma((ND,)), dma((ND,)), dma((ND,)), dma((ND,)), dma((ND,)), dma((ND,)), dma((4,)),
+            pltpu.VMEM((ND, pair, kvw // 2), BF), pltpu.VMEM((ND, pair, kvw // 2), BF),
+            pltpu.VMEM((ND, pair, width), BF), pltpu.VMEM((ND, pair, gw), BF),
+            pltpu.VMEM((ND, pair, kvw // 2), BF), pltpu.VMEM((ND, pair, kvw // 2), BF), pltpu.VMEM((cap, kvw), BF),
+            dma((5,)), dma((ND,)), dma((ND,)), dma((ND,)), dma((ND,)), dma((ND,)), dma((ND,)),
+            dma((ND,)), dma((ND,)), dma((5,)),
             dma((4, 2)), dma((4, 2)), dma((4, 2)), dma((4, 2)),
         ],
         compiler_params=pltpu.CompilerParams(
@@ -286,7 +290,7 @@
 
 
 def attend_kernel(group, kvh, span_ref, tab_ref, all_hbm, rq_hbm, rg_hbm, row_ref, qpos_ref, dkv_hbm, dq_hbm,
-                  all_ref, rq_ref, rg_ref, qs, gs, lse, dlt, dq, dkv, kpos, dkv_ref, dq_ref, ins):
+                  all_ref, rq_ref, rg_ref, qs, gs, lse, dlt, dq, dkv, kpos, dkv_ref, dq_ref, probs, dscore, order, ins):
     nq = qs.shape[1]
     capq = nq * QB
     heads = group * kvh
@@ -328,36 +332,59 @@
             lse[g, i, :, to] = jnp.broadcast_to(stat[heads + h:heads + h + 1, at] * LOG2E, (8, QB))
     loads[2].wait()
 
-    def q_block(i, _):
-        hi = qpos_ref[i, 0:1, :]
-        lo = qpos_ref[i, 1:2, :]
-
-        def k_tile(t, _):
-            rows = pl.ds(pl.multiple_of(t * KS, KS), KS)
-            kp = kpos[:, rows, :].reshape(tile, HDIM)
-            keep = jnp.where((kp <= hi) & (kp >= lo), 1.0, 0.0)
-            keep = jnp.concatenate([keep] * group, axis=1) > 0.5
-            for g in range(kvh):
-                kc = slice(g * HDIM, (g + 1) * HDIM)
-                vc = slice(kvw + g * HDIM, kvw + (g + 1) * HDIM)
-                kt = all_ref[:, rows, kc].reshape(tile, HDIM)
-                vt = all_ref[:, rows, vc].reshape(tile, HDIM)
-                qt = qs[g, i]
-                gt = gs[g, i]
-                last = (((1,), (1,)), ((), ()))
-                s = lax.dot_general(kt, qt, last, preferred_element_type=F32)
-                p = jnp.where(keep, jnp.exp2(s * (scale * LOG2E) - lse[g, i, 0:1, :]), 0.0)
-                dp = lax.dot_general(vt, gt, last, preferred_element_type=F32)
-                ds = (p * (dp - dlt[g, i, 0:1, :]) * scale).astype(BF)
-                dkv[:, rows, vc] += dot(p.astype(BF), gt).reshape(NZ, KS, HDIM)
-                dkv[:, rows, kc] += dot(ds, qt).reshape(NZ, KS, HDIM)
-                dq[g, i] += dot_rows(ds, kt)
-            return 0
-
-        lax.fori_loop(span_ref[0, i], span_ref[1, i], k_tile, 0)
+    def tile_rows(t):
+        return pl.ds(pl.multiple_of(t * KS, KS), KS)
+
+    def weigh(n):
+        i, slot = order[0, n], n % 2
+        rows = tile_rows(order[1, n])
+        kp = kpos[:, rows, :].reshape(tile, HDIM)
+        seen = (kp <= qpos_ref[i, 0:1, :]) & (kp >= qpos_ref[i, 1:2, :])
+        last = (((1,), (1,)), ((), ()))
+        for g in range(kvh):
+            kt = all_ref[:, rows, g * HDIM:(g + 1) * HDIM].reshape(tile, HDIM)
+            vt = all_ref[:, rows, kvw + g * HDIM:kvw + (g + 1) * HDIM].reshape(tile, HDIM)
+            s = lax.dot_general(kt, qs[g, i], last, preferred_element_type=F32)
+            dp = lax.dot_general(vt, gs[g, i], last, preferred_element_type=F32)
+            e = jnp.exp2(s * (scale * LOG2E) - lse[g, i, 0:1, :])
+            p = jnp.concatenate(
+                [jnp.where(seen, e[:, r * QB:(r + 1) * QB], 0.0) for r in range(group)], axis=1)
+            probs[slot, g] = p.astype(BF)
+            dscore[slot, g] = (p * (dp - dlt[g, i, 0:1, :]) * scale).astype(BF)
+
+    def add_up(n):
+        i, slot = order[0, n], n % 2
+        rows = tile_rows(order[1, n])
+        for g in range(kvh):
+            kc = slice(g * HDIM, (g + 1) * HDIM)
+            vc = slice(kvw + g * HDIM, kvw + (g + 1) * HDIM)
+            ds = dscore[slot, g]
+            dkv[:, rows, vc] += dot(probs[slot, g], gs[g, i]).reshape(NZ, KS, HDIM)
+            dkv[:, rows, kc] += dot(ds, qs[g, i]).reshape(NZ, KS, HDIM)
+            dq[g, i] += dot_rows(ds, all_ref[:, rows, kc].reshape(tile, HDIM))
+
+    def list_block(i, n):
+        def list_tile(t, n):
+            order[0, n] = i
+            order[1, n] = t
+            return n + 1
+
+        return lax.fori_loop(span_ref[0, i], span_ref[1, i], list_tile, n)
+
+    total = lax.fori_loop(0, nq, list_block, jnp.int32(0))
+
+    @pl.when(total > 0)
+    def _():
+        weigh(0)
+
+    def step(n, _):
+        add_up(n)
+        weigh(jnp.minimum(n + 1, total))
         return 0
 
-    lax.fori_loop(0, nq, q_block, 0)
+    order[0, total] = 0
+    order[1, total] = 0
+    lax.fori_loop(0, total, step, 0)
     dkv_ref[...] = dkv[...].astype(BF)
     outs = [pltpu.make_async_copy(dkv_ref, dkv_hbm, ins.at[3])]
     outs[0].start()
@@ -393,6 +420,8 @@
             pltpu.VMEM((kvh, nq, group * QB, HDIM), F32), pltpu.VMEM((NZ, cap, kvw), F32),
             pltpu.VMEM((NZ, cap, HDIM), jnp.int32),
             pltpu.VMEM((NZ, cap, kvw), BF), pltpu.VMEM((slots, width), BF),
+            pltpu.VMEM((2, kvh, NZ * KS, group * QB), BF), pltpu.VMEM((2, kvh, NZ * KS, group * QB), BF),
+            pltpu.SMEM((2, nq * (cap // KS) + 1), jnp.int32),
             pltpu.SemaphoreType.DMA((5,)),
         ],
         compiler_params=pltpu.CompilerParams(vmem_limit_bytes=60 << 20),
@@ -401,11 +430,12 @@
 
 
 def return_kernel(dkv_hbm, dq_ref, idx_ref, slot_ref, gq_ref, gk_ref, gv_ref,
-                  dkv_ref, fin, bin_, fout, bout, slots, rdq_ref, rdkv_ref, gq, gk, gv, qs, qr, ks, kr, ls, fs, fr, bs, br):
+                  dkv_ref, fin, bin_, fout, bout, sk, sv, rdq_ref, rk, rv, gq, gk, gv,
+                  qs, qr, ks, kr, vs, vr, ls, fs, fr, bs, br):
     z = lax.axis_index("ctx")
     d = lax.axis_index("dp")
     cap, kvw = dkv_ref.shape[1:]
-    part = cap // 2
+    half_w = kvw // 2
     last = NZ // 2 - 1
     load = pltpu.make_async_copy(dkv_hbm, dkv_ref, ls.at[2])
     load.start()
@@ -413,22 +443,22 @@
     sent = []
 
     def hop(step, piece):
-        rows = pl.ds(piece * part, part)
+        cols = pl.ds(piece * half_w, half_w)
         for by, owner, send, recv, into, out, half in (
                 (1, lax.rem(z + NZ // 2 - step, NZ), fs, fr, fin, fout, 0),
                 (NZ - 1, lax.rem(z + NZ // 2 + step, NZ), bs, br, bin_, bout, 1)):
             if step == 0 and piece != half:
                 continue
             if step == 0 or (step == 1 and piece != half):
-                src = dkv_hbm.at[owner, rows]
+                src = dkv_hbm.at[owner, :, cols]
             else:
                 for s, p, b, c in sent:
                     if s == step - 1 and p == piece and b == by:
                         c.wait_recv()
-                out[step, rows, :] = (dkv_ref[owner, rows, :].astype(F32)
-                                      + into[step - 1, rows, :].astype(F32)).astype(BF)
-                src = out.at[step, rows]
-            c = along(by, src, into.at[step, rows], send.at[step, piece], recv.at[step, piece])
+                out[step, :, cols] = (dkv_ref[owner, :, cols].astype(F32)
+                                      + into[step - 1, :, cols].astype(F32)).astype(BF)
+                src = out.at[step, :, cols]
+            c = along(by, src, into.at[step, :, cols], send.at[step, piece], recv.at[step, piece])
             c.start()
             sent.append((step, piece, by, c))
 
@@ -446,34 +476,36 @@
     own.wait()
     for c in dq_copies:
         c.wait()
-    count, width = slots.shape[0] * slots.shape[1], gq.shape[1]
+    count, width = sk.shape[0] * sk.shape[1], gq.shape[1]
     pick = one_hot_rows(count, slot_ref[...]).T
     rows = rdq_ref[...].reshape(count, width)
     gq[...] = dot(pick, rows).astype(BF)
     outs = [pltpu.make_async_copy(gq, gq_ref, ls.at[3])]
     outs[0].start()
-    for s, p, b, c in sent:
-        if s == last:
-            c.wait_recv()
-    total = (dkv_ref[z].astype(F32) + fin[last].astype(F32) + bin_[last].astype(F32)).astype(BF)
-    slots[...] = dot_rows(one_hot_rows(cap, idx_ref[:, :ND * slots.shape[1]]), total).astype(BF).reshape(slots.shape)
-    kv_copies = exchange(slots, rdkv_ref, ks, kr)
-    for c in kv_copies:
-        c.start()
-    own_kv = pltpu.make_async_copy(slots.at[d], rdkv_ref.at[d], ls.at[1])
-    own_kv.start()
+    spread = one_hot_rows(cap, idx_ref[:, :count])
+    returns = []
+    for piece, (out, into, send, recv) in enumerate(((sk, rk, ks, kr), (sv, rv, vs, vr))):
+        cols = slice(piece * half_w, (piece + 1) * half_w)
+        for s, p, b, c in sent:
+            if s == last and p == piece:
+                c.wait_recv()
+        total = (dkv_ref[z, :, cols].astype(F32) + fin[last, :, cols].astype(F32)
+                 + bin_[last, :, cols].astype(F32)).astype(BF)
+        out[...] = dot_rows(spread, total).astype(BF).reshape(out.shape)
+        copies = exchange(out, into, send, recv)
+        for c in copies:
+            c.start()
+        keep = pltpu.make_async_copy(out.at[d], into.at[d], ls.at[1 + 3 * piece])
+        keep.start()
+        returns.append(copies + [keep])
     for s, p, b, c in sent:
         c.wait_send()
-    own_kv.wait()
-    for c in kv_copies:
-        c.wait()
-    rows = rdkv_ref[...].reshape(count, kvw)
-    gk[...] = dot(pick, rows[:, :kvw // 2]).astype(BF)
-    gv[...] = dot(pick, rows[:, kvw // 2:]).astype(BF)
-    outs.append(pltpu.make_async_copy(gk, gk_ref, ls.at[4]))
-    outs.append(pltpu.make_async_copy(gv, gv_ref, ls.at[5]))
-    for c in outs[1:]:
-        c.start()
+    for piece, (into, stage, dst) in enumerate(((rk, gk, gk_ref), (rv, gv, gv_ref))):
+        for c in returns[piece]:
+            c.wait()
+        stage[...] = dot(pick, into[...].reshape(count, half_w)).astype(BF)
+        outs.append(pltpu.make_async_copy(stage, dst, ls.at[5 + piece]))
+        outs[-1].start()
     for c in outs:
         c.wait()
 
@@ -493,9 +525,11 @@
         in_specs=[ANY_SPEC, ANY_SPEC, VMEM_SPEC, VMEM_SPEC],
         out_specs=(ANY_SPEC,) * 3,
         scratch_shapes=[pltpu.VMEM((NZ, cap, kvw), BF)] + [pltpu.VMEM((NZ // 2, cap, kvw), BF)] * 4 + [
-            pltpu.VMEM((ND, pair, kvw), BF), pltpu.VMEM((ND, pair, width), BF), pltpu.VMEM((ND, pair, kvw), BF),
+            pltpu.VMEM((ND, pair, kvw // 2), BF), pltpu.VMEM((ND, pair, kvw // 2), BF),
+            pltpu.VMEM((ND, pair, width), BF),
+            pltpu.VMEM((ND, pair, kvw // 2), BF), pltpu.VMEM((ND, pair, kvw // 2), BF),
             pltpu.VMEM((tok, width), BF), pltpu.VMEM((tok, kvw // 2), BF), pltpu.VMEM((tok, kvw // 2), BF),
-            dma((ND,)), dma((ND,)), dma((ND,)), dma((ND,)), dma((6,)),
+            dma((ND,)), dma((ND,)), dma((ND,)), dma((ND,)), dma((ND,)), dma((ND,)), dma((7,)),
             dma((4, 2)), dma((4, 2)), dma((4, 2)), dma((4, 2)),
         ],
         compiler_params=pltpu.CompilerParams(

time: 163 us -> 159 us (0.975)
  Pallas kernels: 158 us -> 154 us
    pallas_call x1, Pallas kernels: 47.3 us -> 57.9 us  [send_back(): pl.pallas_call(return_kernel, out_shape=(jax.ShapeDtypeStruct((tok, width...]
    pallas_call x1, Pallas kernels: 41.4 us -> 32.4 us  [attend(): pl.pallas_call(functools.partial(attend_kernel, group, kvh), out_shape=(j...]
    pallas_call x1, Pallas kernels: 65.2 us -> 60.2 us  [dispatch(): pl.pallas_call(dispatch_kernel, out_shape=(jax.ShapeDtypeStruct((NZ, cap,...]
where the time goes in v5:
time: 159 us
  Pallas kernels  154 us (97%)
  local copies, waits for them, and re-layouts  2.26 us (1%)
    pallas_call x1, Pallas kernels, dispatch(): pl.pallas_call(dispatch_kernel, out_shape=(jax.ShapeDtypeStruct((NZ, cap,...  60.2 us
    pallas_call x1, Pallas kernels, send_back(): pl.pallas_call(return_kernel, out_shape=(jax.ShapeDtypeStruct((tok, width...  57.9 us
    pallas_call x1, Pallas kernels, attend(): pl.pallas_call(functools.partial(attend_kernel, group, kvh), out_shape=(j...  32.4 us
    pallas_call x1, Pallas kernels, tables(): pl.pallas_call(functools.partial(tables_kernel, tok), out_shape=(jax.Shap...  3.91 us

profile of v5, /device:TPU:4, one launch (start us, length us, event | category | flops | bytes accessed | tf_op | source)
XLA Modules:
  0.0 158.6 jit_solution(3849659347205469398)
XLA Ops:
  0.6 3.9 %routing_tables.1 = (s32[1,352]{1,0:T(1,128)S(1)}, s32[1,704]{1,0:T(1,128)S(1)}, s32[6,2,128]{2,1,0:T(2,128)S(1)}, s32[8,16]{1,0:T(8,128)S(1)}, s32[2,6]{1,0:T(2,128)S(1)}, /*index=5*/s32[1]{0:T(128)}) custom-call(s32[64,64]{1,0:T(8,128)} %counts_ref.1, s32[64,64]{1,0:T(8,128)} %counts_ref.1, s32[1,4]{1,0:T(1,128)} %doc_ref.1), custom_call_target="tpu_custom_call" | custom-call | tf_op jit(solution)/shard_map/routing_tables/pallas_call | solution.py:124
  5.2 151.1 %conditional.1 = ((bf16[352,1280]{1,0:T(8,128)(2,1)S(1)}, bf16[352,256]{1,0:T(8,128)(2,1)S(1)}, bf16[352,256]{1,0:T(8,128)(2,1)S(1)})) conditional(s32[]{:T(128)} %bitcast.8, (bf16[352,10]{0,1:T(8,128)(2,1)}, bf16[352,1280]{1,0:T(8,128)(2,1)}, bf16[352,256]{1,0:T(8,128)(2,1)}, bf16[352,256]{1,0:T(8,128)(2,1)}, bf16[352,1280]{1,0:T(8,128)(2,1)}, ...), branch_computations={%region_0.0_spmd, %region_1.0_spmd} | conditional | bytes 8 | solution.py:554
  5.4 60.2 %dispatch_rows.3 = (bf16[8,448,512]{2,1,0:T(8,128)(2,1)}, bf16[8,80,1280]{2,1,0:T(8,128)(2,1)}, bf16[8,80,1408]{2,1,0:T(8,128)(2,1)}) custom-call(bf16[352,1280]{1,0:T(8,128)(2,1)} %get-tuple-element.62.q_ref, bf16[352,256]{1,0:T(8,128)(2,1)} %get-tuple-element.63.k_ref, bf16[352,256]{1,0:T(8,128)(2,1)} %get-tuple-element.64.v_ref, ...), custom_call_target="tpu_custom_call" | custom-call | tf_op jit(solution)/shard_map/cond/branch_1_fun/dispatch_rows/pallas_call | solution.py:267
  65.7 32.4 %attention_grads.3 = (bf16[8,448,512]{2,1,0:T(8,128)(2,1)}, bf16[640,1280]{1,0:T(8,128)(2,1)}) custom-call(s32[2,6]{1,0:T(2,128)S(1)} %get-tuple-element.60.span_ref, s32[8,16]{1,0:T(8,128)S(1)} %get-tuple-element.61.tab_ref, bf16[8,448,512]{2,1,0:T(8,128)(2,1)} %get-tuple-element.70.all_hbm, bf16[640,1280]{1,0:T(8,128)(2,1)} %bitcast.14, ...), custom_call_target="tpu_custom_call" | custom-call | tf_op jit(solution)/shard_map/cond/branch_1_fun/attention_grads/pallas_call | solution.py:408
  98.1 57.9 %return_rows.3 = (bf16[352,1280]{1,0:T(8,128)(2,1)S(1)}, bf16[352,256]{1,0:T(8,128)(2,1)S(1)}, bf16[352,256]{1,0:T(8,128)(2,1)S(1)}) custom-call(bf16[8,448,512]{2,1,0:T(8,128)(2,1)} %get-tuple-element.74.dkv_hbm, bf16[8,80,1280]{2,1,0:T(8,128)(2,1)} %bitcast.13, s32[1,704]{1,0:T(1,128)S(1)} %get-tuple-element.69.idx_ref.row_ref, ...), custom_call_target="tpu_custom_call" | custom-call | tf_op jit(solution)/shard_map/cond/branch_1_fun/return_rows/pallas_call | solution.py:518
  156.3 0.9 copy.26
  157.3 0.7 copy.27
  157.9 0.7 copy.28

commit v6 on v5

--- a/solution.py
+++ b/solution.py
@@ -16,6 +16,7 @@
 SLOW = (704, 88)
 FAR = 1 << 20
 LOG2E = 1.4426950408889634
+CROSS_FIRST = (6, 5, 7, 4, 2, 1, 3)
 MESH = pl.DeviceIdType.MESH
 BF = jnp.bfloat16
 F32 = jnp.float32
@@ -149,8 +150,8 @@
 def exchange(src, dst, send, recv):
     d = lax.axis_index("dp")
     copies = []
-    for s in range(1, ND):
-        to = lax.rem(d + s, ND)
+    for s in CROSS_FIRST:
+        to = lax.rem(d // 4 + s // 4, 2) * 4 + lax.rem(d + s, 4)
         copies.append(pltpu.make_async_remote_copy(
             src_ref=src.at[to], dst_ref=dst.at[d], send_sem=send.at[s], recv_sem=recv.at[s],
             device_id={"dp": to}, device_id_type=MESH))
@@ -361,7 +362,7 @@
             ds = dscore[slot, g]
             dkv[:, rows, vc] += dot(probs[slot, g], gs[g, i]).reshape(NZ, KS, HDIM)
             dkv[:, rows, kc] += dot(ds, qs[g, i]).reshape(NZ, KS, HDIM)
-            dq[g, i] += dot_rows(ds, all_ref[:, rows, kc].reshape(tile, HDIM))
+            dq[g, i] += dot_rows(all_ref[:, rows, kc].reshape(tile, HDIM), ds)
 
     def list_block(i, n):
         def list_tile(t, n):
@@ -393,8 +394,10 @@
         cols = []
         for e in range(2):
             g, r = divmod(h + e, group)
-            cols.append(jnp.concatenate([dq[g, i, r * QB:(r + 1) * QB, :] for i in range(nq)], axis=0).astype(BF))
-        dq_ref[:, h * HDIM:(h + 2) * HDIM] = dot(back, jnp.concatenate(cols, axis=1)).astype(BF)
+            cols.append(jnp.concatenate([dq[g, i, :, r * QB:(r + 1) * QB] for i in range(nq)], axis=1).astype(BF))
+        both = lax.dot_general(back, jnp.concatenate(cols, axis=0), (((1,), (1,)), ((), ())),
+                               preferred_element_type=F32)
+        dq_ref[:, h * HDIM:(h + 2) * HDIM] = both.astype(BF)
     outs.append(pltpu.make_async_copy(dq_ref, dq_hbm, ins.at[4]))
     outs[1].start()
     for c in outs:
@@ -417,7 +420,7 @@
             pltpu.VMEM((NZ, cap, kvw), BF), pltpu.VMEM(rq.shape, BF), pltpu.VMEM(rg.shape, BF),
             pltpu.VMEM((kvh, nq, group * QB, HDIM), BF), pltpu.VMEM((kvh, nq, group * QB, HDIM), BF),
             pltpu.VMEM((kvh, nq, 8, group * QB), F32), pltpu.VMEM((kvh, nq, 8, group * QB), F32),
-            pltpu.VMEM((kvh, nq, group * QB, HDIM), F32), pltpu.VMEM((NZ, cap, kvw), F32),
+            pltpu.VMEM((kvh, nq, HDIM, group * QB), F32), pltpu.VMEM((NZ, cap, kvw), F32),
             pltpu.VMEM((NZ, cap, HDIM), jnp.int32),
             pltpu.VMEM((NZ, cap, kvw), BF), pltpu.VMEM((slots, width), BF),
             pltpu.VMEM((2, kvh, NZ * KS, group * QB), BF), pltpu.VMEM((2, kvh, NZ * KS, group * QB), BF),

time: 159 us -> 150 us (0.943)
  Pallas kernels: 154 us -> 144 us
    pallas_call x1, Pallas kernels: 57.9 us -> 53.3 us  [send_back(): pl.pallas_call(return_kernel, out_shape=(jax.ShapeDtypeStruct((tok, width...]
    pallas_call x1, Pallas kernels: 32.4 us -> 29.5 us  [attend(): pl.pallas_call(functools.partial(attend_kernel, group, kvh), out_shape=(j...]
    pallas_call x1, Pallas kernels: 60.2 us -> 57.5 us  [dispatch(): pl.pallas_call(dispatch_kernel, out_shape=(jax.ShapeDtypeStruct((NZ, cap,...]
where the time goes in v6:
time: 150 us; the launch traced here: 148 us
  Pallas kernels  144 us (96%)
  local copies, waits for them, and re-layouts  2.26 us (2%)
    pallas_call x1, Pallas kernels, dispatch(): pl.pallas_call(dispatch_kernel, out_shape=(jax.ShapeDtypeStruct((NZ, cap,...  57.5 us
    pallas_call x1, Pallas kernels, send_back(): pl.pallas_call(return_kernel, out_shape=(jax.ShapeDtypeStruct((tok, width...  53.3 us
    pallas_call x1, Pallas kernels, attend(): pl.pallas_call(functools.partial(attend_kernel, group, kvh), out_shape=(j...  29.5 us
    pallas_call x1, Pallas kernels, tables(): pl.pallas_call(functools.partial(tables_kernel, tok), out_shape=(jax.Shap...  3.91 us

profile of v6, /device:TPU:4, one launch (start us, length us, event | category | flops | bytes accessed | tf_op | source)
XLA Modules:
  0.0 148.3 jit_solution(6700607754374446736)
XLA Ops:
  0.6 3.9 %routing_tables.1 = (s32[1,352]{1,0:T(1,128)S(1)}, s32[1,704]{1,0:T(1,128)S(1)}, s32[6,2,128]{2,1,0:T(2,128)S(1)}, s32[8,16]{1,0:T(8,128)S(1)}, s32[2,6]{1,0:T(2,128)S(1)}, /*index=5*/s32[1]{0:T(128)}) custom-call(s32[64,64]{1,0:T(8,128)} %counts_ref.1, s32[64,64]{1,0:T(8,128)} %counts_ref.1, s32[1,4]{1,0:T(1,128)} %doc_ref.1), custom_call_target="tpu_custom_call" | custom-call | tf_op jit(solution)/shard_map/routing_tables/pallas_call | solution.py:125
  5.2 140.8 %conditional.1 = ((bf16[352,1280]{1,0:T(8,128)(2,1)S(1)}, bf16[352,256]{1,0:T(8,128)(2,1)S(1)}, bf16[352,256]{1,0:T(8,128)(2,1)S(1)})) conditional(s32[]{:T(128)} %bitcast.8, (bf16[352,10]{0,1:T(8,128)(2,1)}, bf16[352,1280]{1,0:T(8,128)(2,1)}, bf16[352,256]{1,0:T(8,128)(2,1)}, bf16[352,256]{1,0:T(8,128)(2,1)}, bf16[352,1280]{1,0:T(8,128)(2,1)}, ...), branch_computations={%region_0.0_spmd, %region_1.0_spmd} | conditional | bytes 8 | solution.py:557
  5.4 57.5 %dispatch_rows.3 = (bf16[8,448,512]{2,1,0:T(8,128)(2,1)}, bf16[8,80,1280]{2,1,0:T(8,128)(2,1)}, bf16[8,80,1408]{2,1,0:T(8,128)(2,1)}) custom-call(bf16[352,1280]{1,0:T(8,128)(2,1)} %get-tuple-element.62.q_ref, bf16[352,256]{1,0:T(8,128)(2,1)} %get-tuple-element.63.k_ref, bf16[352,256]{1,0:T(8,128)(2,1)} %get-tuple-element.64.v_ref, ...), custom_call_target="tpu_custom_call" | custom-call | tf_op jit(solution)/shard_map/cond/branch_1_fun/dispatch_rows/pallas_call | solution.py:268
  62.9 29.5 %attention_grads.3 = (bf16[8,448,512]{2,1,0:T(8,128)(2,1)}, bf16[640,1280]{1,0:T(8,128)(2,1)}) custom-call(s32[2,6]{1,0:T(2,128)S(1)} %get-tuple-element.60.span_ref, s32[8,16]{1,0:T(8,128)S(1)} %get-tuple-element.61.tab_ref, bf16[8,448,512]{2,1,0:T(8,128)(2,1)} %get-tuple-element.70.all_hbm, bf16[640,1280]{1,0:T(8,128)(2,1)} %bitcast.14, ...), custom_call_target="tpu_custom_call" | custom-call | tf_op jit(solution)/shard_map/cond/branch_1_fun/attention_grads/pallas_call | solution.py:411
  92.4 53.3 %return_rows.3 = (bf16[352,1280]{1,0:T(8,128)(2,1)S(1)}, bf16[352,256]{1,0:T(8,128)(2,1)S(1)}, bf16[352,256]{1,0:T(8,128)(2,1)S(1)}) custom-call(bf16[8,448,512]{2,1,0:T(8,128)(2,1)} %get-tuple-element.74.dkv_hbm, bf16[8,80,1280]{2,1,0:T(8,128)(2,1)} %bitcast.13, s32[1,704]{1,0:T(1,128)S(1)} %get-tuple-element.69.idx_ref.row_ref, ...), custom_call_target="tpu_custom_call" | custom-call | tf_op jit(solution)/shard_map/cond/branch_1_fun/return_rows/pallas_call | solution.py:521
  146.0 0.9 copy.26
  147.0 0.7 copy.27
  147.6 0.7 copy.28

commit v7 on v6

--- a/solution.py
+++ b/solution.py
@@ -541,6 +541,33 @@
     )(dkv, dq, idx_row, slot_row)
 
 
+def hand_over_kernel(*refs):
+    count = (len(refs) - 1) // 2
+    sems = refs[-1]
+    copies = []
+    for n in range(count):
+        half = refs[n].shape[0] // 2
+        for part in range(2):
+            rows = pl.ds(part * half, half)
+            copies.append(pltpu.make_async_copy(
+                refs[n].at[rows], refs[count + n].at[rows], sems.at[2 * n + part]))
+    for c in copies:
+        c.start()
+    for c in copies:
+        c.wait()
+
+
+def hand_over(arrays):
+    return pl.pallas_call(
+        hand_over_kernel,
+        out_shape=tuple(jax.ShapeDtypeStruct(a.shape, a.dtype) for a in arrays),
+        in_specs=[ANY_SPEC] * len(arrays),
+        out_specs=(ANY_SPEC,) * len(arrays),
+        scratch_shapes=[pltpu.SemaphoreType.DMA((2 * len(arrays),))],
+        name="hand_over",
+    )(*arrays)
+
+
 def body(query, keys, values, output, grad_out, log_norm, route_counts, doc_lengths):
     tok = query.shape[0]
     kvh = keys.shape[1] // HDIM
@@ -552,7 +579,7 @@
         slots = ND * pair
         kv_all, rq, rg = dispatch(*rows, slot, idx, cap, pair, cid)
         dkv, dq = attend(span, tab, kv_all, rq.reshape(slots, -1), rg.reshape(slots, -1), idx, qpos, group, kvh)
-        return send_back(dkv, dq.reshape(ND, pair, -1), idx, slot, cid + 1)
+        return hand_over(send_back(dkv, dq.reshape(ND, pair, -1), idx, slot, cid + 1))
 
     return lax.cond(fits[0] > 0, functools.partial(run, FAST, 0), functools.partial(run, SLOW, 2),
                     query, keys, values, output, grad_out, log_norm)

time: 150 us -> 188 us (1.25)
  Pallas kernels: 144 us -> 185 us
  local copies, waits for them, and re-layouts: 2.26 us -> 0 us
    pallas_call x0 -> x1, Pallas kernels: none -> 39.4 us  [hand_over(): pl.pallas_call(hand_over_kernel, out_shape=tuple((jax.ShapeDtypeStruct(a....]
    pallas_call x1, Pallas kernels: 29.5 us -> 34.5 us  [attend(): pl.pallas_call(functools.partial(attend_kernel, group, kvh), out_shape=(j...]
    pallas_call x1, Pallas kernels: 53.3 us -> 49.9 us  [send_back(): pl.pallas_call(return_kernel, out_shape=(jax.ShapeDtypeStruct((tok, width...]
    unnamed x3 -> x0, local copies, waits for them, and re-layouts: 2.26 us -> none
where the time goes in v7:
time: 188 us; the launch traced here: 187 us
  Pallas kernels  185 us (98%)
    pallas_call x1, Pallas kernels, dispatch(): pl.pallas_call(dispatch_kernel, out_shape=(jax.ShapeDtypeStruct((NZ, cap,...  57.5 us
    pallas_call x1, Pallas kernels, send_back(): pl.pallas_call(return_kernel, out_shape=(jax.ShapeDtypeStruct((tok, width...  49.9 us
    pallas_call x1, Pallas kernels, hand_over(): pl.pallas_call(hand_over_kernel, out_shape=tuple((jax.ShapeDtypeStruct(a....  39.4 us
    pallas_call x1, Pallas kernels, attend(): pl.pallas_call(functools.partial(attend_kernel, group, kvh), out_shape=(j...  34.5 us
    pallas_call x1, Pallas kernels, tables(): pl.pallas_call(functools.partial(tables_kernel, tok), out_shape=(jax.Shap...  3.91 us

profile of v7, /device:TPU:4, one launch (start us, length us, event | category | flops | bytes accessed | tf_op | source)
XLA Modules:
  0.0 187.2 jit_solution(11653812982830839830)
XLA Ops:
  0.6 3.9 %routing_tables.1 = (s32[1,352]{1,0:T(1,128)S(1)}, s32[1,704]{1,0:T(1,128)S(1)}, s32[6,2,128]{2,1,0:T(2,128)S(1)}, s32[8,16]{1,0:T(8,128)S(1)}, s32[2,6]{1,0:T(2,128)S(1)}, /*index=5*/s32[1]{0:T(128)}) custom-call(s32[64,64]{1,0:T(8,128)} %counts_ref.1, s32[64,64]{1,0:T(8,128)} %counts_ref.1, s32[1,4]{1,0:T(1,128)} %doc_ref.1), custom_call_target="tpu_custom_call" | custom-call | tf_op jit(solution)/shard_map/routing_tables/pallas_call | solution.py:125
  5.2 181.8 %conditional.1 = ((bf16[352,1280]{1,0:T(8,128)(2,1)}, bf16[352,256]{1,0:T(8,128)(2,1)}, bf16[352,256]{1,0:T(8,128)(2,1)})) conditional(s32[]{:T(128)} %bitcast.8, (bf16[352,10]{0,1:T(8,128)(2,1)}, bf16[352,1280]{1,0:T(8,128)(2,1)}, bf16[352,256]{1,0:T(8,128)(2,1)}, bf16[352,256]{1,0:T(8,128)(2,1)}, bf16[352,1280]{1,0:T(8,128)(2,1)}, ...), branch_computations={%region_0.0_spmd, %region_1.0_spmd} | conditional | bytes 8 | solution.py:584
  5.4 57.5 %dispatch_rows.3 = (bf16[8,448,512]{2,1,0:T(8,128)(2,1)}, bf16[8,80,1280]{2,1,0:T(8,128)(2,1)}, bf16[8,80,1408]{2,1,0:T(8,128)(2,1)}) custom-call(bf16[352,1280]{1,0:T(8,128)(2,1)} %get-tuple-element.65.q_ref, bf16[352,256]{1,0:T(8,128)(2,1)} %get-tuple-element.66.k_ref, bf16[352,256]{1,0:T(8,128)(2,1)} %get-tuple-element.67.v_ref, ...), custom_call_target="tpu_custom_call" | custom-call | tf_op jit(solution)/shard_map/cond/branch_1_fun/dispatch_rows/pallas_call | solution.py:268
  62.9 34.5 %attention_grads.3 = (bf16[8,448,512]{2,1,0:T(8,128)(2,1)}, bf16[640,1280]{1,0:T(8,128)(2,1)}) custom-call(s32[2,6]{1,0:T(2,128)S(1)} %get-tuple-element.63.span_ref, s32[8,16]{1,0:T(8,128)S(1)} %get-tuple-element.64.tab_ref, bf16[8,448,512]{2,1,0:T(8,128)(2,1)} %get-tuple-element.73.all_hbm, bf16[640,1280]{1,0:T(8,128)(2,1)} %bitcast.14, ...), custom_call_target="tpu_custom_call" | custom-call | tf_op jit(solution)/shard_map/cond/branch_1_fun/attention_grads/pallas_call | solution.py:411
  97.4 49.9 %return_rows.3 = (bf16[352,1280]{1,0:T(8,128)(2,1)}, bf16[352,256]{1,0:T(8,128)(2,1)}, bf16[352,256]{1,0:T(8,128)(2,1)}) custom-call(bf16[8,448,512]{2,1,0:T(8,128)(2,1)} %get-tuple-element.77.dkv_hbm, bf16[8,80,1280]{2,1,0:T(8,128)(2,1)} %bitcast.13, s32[1,704]{1,0:T(1,128)S(1)} %get-tuple-element.72.idx_ref.row_ref, s32[1,352]{1,0:T(1,128)S(1)} %get-tuple-element.71.slot_ref), custom_call_target="tpu_custom_call" | custom-call | tf_op jit(solution)/shard_map/cond/branch_1_fun/return_rows/pallas_call | solution.py:521
  147.3 39.4 %hand_over.3 = (bf16[352,1280]{1,0:T(8,128)(2,1)}, bf16[352,256]{1,0:T(8,128)(2,1)}, bf16[352,256]{1,0:T(8,128)(2,1)}) custom-call(bf16[352,1280]{1,0:T(8,128)(2,1)} %get-tuple-element.79.refs_0_, bf16[352,256]{1,0:T(8,128)(2,1)} %get-tuple-element.80.refs_1_, bf16[352,256]{1,0:T(8,128)(2,1)} %get-tuple-element.81.refs_2_), custom_call_target="tpu_custom_call" | custom-call | tf_op jit(solution)/shard_map/cond/branch_1_fun/hand_over/pallas_call | solution.py:561
